TPU v7x, 256 devices: a whole 4x4x8 slice. The times are simulated.
256 devices in a mesh: seq: 8 (over y, core), expert: 16 (over x_hi, z), rep: 2 (over x_lo).
Axes of the slice: x: 4 (x_hi: 2, x_lo: 2; x = x_hi * 2 + x_lo), y: 4, z: 8, core: 2. Of those that a mesh axis runs over, the one named last changes fastest.
Arguments:
- tokens: bfloat16 [2, 1024, 4096], P(None, ('seq', 'expert', 'rep')), may hold values from -6 to 6
- grad_out: bfloat16 [2, 1024, 4096], P(None, ('seq', 'expert', 'rep')), may hold values from -6 to 6
- expert_ids: int32 [2, 1024, 8], P(None, ('seq', 'expert', 'rep')), may hold values from 0 to 15, all different within a row; in each aligned block of 4 rows (0 to 3, 4 to 7, ..., all dimensions but the last counted through in order) at most 3 rows name the same one
- gate_weights: bfloat16 [2, 1024, 8], P(None, ('seq', 'expert', 'rep')), may hold values from 0.25 to 1
- w_gate: bfloat16 [16, 1536, 4096], P('expert', 'seq'), may hold values from -0.09375 to 0.09375
- w_up: bfloat16 [16, 1536, 4096], P('expert', 'seq'), may hold values from -0.09375 to 0.09375
- w_down: bfloat16 [16, 1536, 4096], P('expert', 'seq'), may hold values from -0.15625 to 0.15625
Outputs:
- d_tokens: bfloat16 [2, 1024, 4096], P(None, ('seq', 'expert', 'rep'))
- grad_gate: bfloat16 [16, 1536, 4096], P('expert', 'seq')
- grad_up: bfloat16 [16, 1536, 4096], P('expert', 'seq')
- grad_down: bfloat16 [16, 1536, 4096], P('expert', 'seq')
Inputs may be any that keep to these rules, and one draw needn't show every extreme that they name: `expert_ids`: in each aligned block of 4 rows (the rows of one device in one micro-batch) a row names 8 different experts, and no expert is named by more than 3 rows of the block; some expert is named by exactly 3 rows in some blocks.
All inputs are finite; a program needn't handle non-finite values.
Results may differ from a plain program's by a relative error of at most 0.019.
Values may be sent and summed in bfloat16 or wider, within the bound.
A program may use at most 128 MiB of HBM per device.

v0:
```python
import jax
import jax.numpy as jnp
from jax import lax
from jax.sharding import PartitionSpec as P


def capacity_of(block_rows, top_count, experts):
    return min(block_rows, max(2, (block_rows * top_count + experts - 1) // experts * 3 // 2))


def slot_table(block_ids, experts, capacity):
    flat = block_ids.reshape(-1)
    entries = flat.shape[0]
    onehot = (flat[:, None] == jnp.arange(experts, dtype=jnp.int32)[None, :]).astype(jnp.int32)
    before = jnp.cumsum(onehot, axis=0) - onehot
    ranking = jnp.sum(before * onehot, axis=1)
    position = flat * capacity + ranking
    source = jnp.full((experts * capacity,), entries, jnp.int32)
    source = source.at[position].set(jnp.arange(entries, dtype=jnp.int32))
    return (source, source < entries, position)


def fill_slots(rows_in, rows_grad, block_gates, source, filled):
    top_count = block_gates.shape[1]
    clipped = jnp.minimum(source, rows_in.shape[0] * top_count - 1)
    token_at = clipped // top_count
    in_slots = jnp.where(filled[:, None], rows_in[token_at], jnp.zeros((), rows_in.dtype))
    weight_at = jnp.where(filled, block_gates.reshape(-1)[clipped].astype(jnp.float32), 0.0)
    grad_slots = (weight_at[:, None] * rows_grad[token_at].astype(jnp.float32)).astype(jnp.bfloat16)
    return (in_slots, grad_slots)


def gather_back(slot_values, position, block_rows, top_count):
    picked = slot_values[position]
    return jnp.sum(picked.reshape(block_rows, top_count, slot_values.shape[1]), axis=1)


def expert_forward(in_rows, grad_rows, gate_rows, up_rows, down_rows):
    gate_pre = jnp.einsum("nd,fd->nf", in_rows, gate_rows, preferred_element_type=jnp.float32)
    up_pre = jnp.einsum("nd,fd->nf", in_rows, up_rows, preferred_element_type=jnp.float32)
    sigma = jax.nn.sigmoid(gate_pre)
    active = gate_pre * sigma
    hidden = (active * up_pre).astype(jnp.bfloat16)
    d_hidden = jnp.einsum("nd,fd->nf", grad_rows, down_rows, preferred_element_type=jnp.float32)
    d_up = (d_hidden * active).astype(jnp.bfloat16)
    d_gate = (d_hidden * up_pre * sigma * (1.0 + gate_pre * (1.0 - sigma))).astype(jnp.bfloat16)
    return (d_gate, d_up, hidden)


def input_terms(d_gate, d_up, gate_rows, up_rows):
    first = jnp.einsum("nf,fd->nd", d_gate, gate_rows, preferred_element_type=jnp.float32)
    return first + jnp.einsum("nf,fd->nd", d_up, up_rows, preferred_element_type=jnp.float32)


def body(tokens, grad_out, expert_ids, gate_weights, w_gate, w_up, w_down):
    seq_count = lax.axis_size("seq")
    experts = lax.axis_size("expert")
    micro_count, block_rows, top_count = expert_ids.shape
    width = tokens.shape[2]
    capacity = capacity_of(block_rows, top_count, experts)
    slots = experts * capacity
    gate_rows = w_gate[0]
    up_rows = w_up[0]
    down_rows = w_down[0]

    def table_of(block_ids):
        source, filled, position = slot_table(block_ids, experts, capacity)
        return (source, filled)

    group_ids = lax.all_gather(expert_ids, "seq", axis=1, tiled=True)
    results = []
    kept_in = []
    kept_grad = []
    kept_gate = []
    kept_up = []
    kept_hidden = []
    for micro in range(micro_count):
        own_source, own_filled, own_position = slot_table(expert_ids[micro], experts, capacity)
        group_in, group_grad, group_gates = (
            lax.all_gather(tokens[micro], "seq", axis=0, tiled=True),
            lax.all_gather(grad_out[micro], "seq", axis=0, tiled=True),
            lax.all_gather(gate_weights[micro], "seq", axis=0, tiled=True),
        )
        block_ids = group_ids[micro].reshape(seq_count, block_rows, top_count)
        sources, filleds = jax.vmap(table_of)(block_ids)
        in_send, grad_send = jax.vmap(fill_slots)(
            group_in.reshape(seq_count, block_rows, width),
            group_grad.reshape(seq_count, block_rows, width),
            group_gates.reshape(seq_count, block_rows, top_count),
            sources,
            filleds,
        )
        in_recv, grad_recv = (
            lax.all_to_all(
                in_send.reshape(seq_count, experts, capacity, width),
                "expert",
                split_axis=1,
                concat_axis=1,
                tiled=True,
            ),
            lax.all_to_all(
                grad_send.reshape(seq_count, experts, capacity, width),
                "expert",
                split_axis=1,
                concat_axis=1,
                tiled=True,
            ),
        )
        in_rows = in_recv.reshape(-1, width)
        grad_rows = grad_recv.reshape(-1, width)
        d_gate, d_up, hidden = expert_forward(in_rows, grad_rows, gate_rows, up_rows, down_rows)
        kept_in.append(in_rows)
        kept_grad.append(grad_rows)
        kept_gate.append(d_gate)
        kept_up.append(d_up)
        kept_hidden.append(hidden)
        pieces = input_terms(d_gate, d_up, gate_rows, up_rows).astype(jnp.bfloat16)
        returned = lax.all_to_all(
            pieces.reshape(seq_count, experts, capacity, width),
            "expert",
            split_axis=1,
            concat_axis=1,
            tiled=True,
        )
        summed = lax.psum_scatter(returned, "seq", scatter_dimension=0, tiled=True).astype(
            jnp.float32
        )[0]
        d_block = gather_back(summed.reshape(slots, width), own_position, block_rows, top_count)
        results.append(d_block.astype(jnp.bfloat16))
    all_in = jnp.concatenate(kept_in, axis=0)
    all_grad = jnp.concatenate(kept_grad, axis=0)
    all_gate = jnp.concatenate(kept_gate, axis=0)
    all_up = jnp.concatenate(kept_up, axis=0)
    all_hidden = jnp.concatenate(kept_hidden, axis=0)
    total_gate = jnp.einsum("nf,nd->fd", all_gate, all_in, preferred_element_type=jnp.float32)
    total_up = jnp.einsum("nf,nd->fd", all_up, all_in, preferred_element_type=jnp.float32)
    total_down = jnp.einsum("nf,nd->fd", all_hidden, all_grad, preferred_element_type=jnp.float32)
    sum_gate, sum_up, sum_down = (
        lax.psum(total_gate.astype(jnp.bfloat16), "rep").astype(jnp.float32),
        lax.psum(total_up.astype(jnp.bfloat16), "rep").astype(jnp.float32),
        lax.psum(total_down.astype(jnp.bfloat16), "rep").astype(jnp.float32),
    )
    grad_gate = sum_gate.astype(jnp.bfloat16)[None]
    grad_up = sum_up.astype(jnp.bfloat16)[None]
    grad_down = sum_down.astype(jnp.bfloat16)[None]
    return (jnp.stack(results), grad_gate, grad_up, grad_down)


def solution(mesh):
    return jax.shard_map(
        body,
        mesh=mesh,
        in_specs=(
            P(None, ("seq", "expert", "rep"), None),
            P(None, ("seq", "expert", "rep"), None),
            P(None, ("seq", "expert", "rep"), None),
            P(None, ("seq", "expert", "rep"), None),
            P("expert", "seq", None),
            P("expert", "seq", None),
            P("expert", "seq", None),
        ),
        out_specs=(
            P(None, ("seq", "expert", "rep"), None),
            P("expert", "seq", None),
            P("expert", "seq", None),
            P("expert", "seq", None),
        ),
        check_vma=False,
    )
```

profile of v0, /device:TPU:1, one launch (start us, length us, event | category | flops | bytes accessed | tf_op | source)
XLA Modules:
  0.0 776.3 jit_solution(14246266803586308784)
XLA Ops:
  8.8 15.8 %all_gather.21 = s32[2,32,8]{2,0,1:T(2,128)S(1)} all-gather(s32[2,4,8]{2,0,1:T(2,128)S(1)} %copy.56), channel_id=1, replica_groups=mesh['seq'=8,'expert'=16,'rep'=2] {'seq'}, dimensions={1}, use_global_device_ids=true | all-gather | bytes 2304 | tf_op jit(solution)/shard_map/all_gather | solution.py:70
  26.2 11.2 %scatter_fusion = s32[8,48]{1,0:T(8,128)S(1)} fusion(s32[8,48]{1,0:T(8,128)S(1)} %broadcast.147.clone.1, s32[256]{0:T(256)S(1)} %reshape.268, s32[256]{0:T(256)S(1)} %reshape.270), kind=kCustom, calls=%fused_computation.8 | custom fusion | bytes 5120 | tf_op jit(solution)/shard_map/vmap()/scatter | solution.py:19
  37.5 11.2 %all-gather = bf16[1,32,8]{2,0,1:T(2,128)(2,1)S(1)} all-gather(bf16[1,4,8]{2,0,1:T(2,128)(2,1)S(1)} %copy.99), channel_id=2, replica_groups=mesh['seq'=8,'expert'=16,'rep'=2] {'seq'}, dimensions={1}, use_global_device_ids=true | all-gather | bytes 576 | tf_op jit(solution)/shard_map/all_gather | solution.py:82
  52.8 13.4 %all-gather.2 = bf16[1,32,4096]{2,0,1:T(2,128)(2,1)S(1)} all-gather(bf16[1,4,4096]{2,0,1:T(2,128)(2,1)S(1)} %copy.101), channel_id=4, replica_groups=mesh['seq'=8,'expert'=16,'rep'=2] {'seq'}, dimensions={1}, use_global_device_ids=true | all-gather | bytes 294912 | tf_op jit(solution)/shard_map/all_gather | solution.py:80
  67.9 16.3 %gather_fusion.4 = bf16[384,4096]{1,0:T(8,128)(2,1)} fusion(bf16[8,4,4096]{2,1,0:T(4,128)(2,1)S(1)} %reshape.202, s32[384]{0:T(512)S(1)} %reshape.238), kind=kCustom, calls=%fused_computation.4 | custom fusion | bytes 6294528 | tf_op jit(solution)/shard_map/vmap()/gather | solution.py:27
  100.3 9.7 %all-to-all-start.1 = ((bf16[8,16,3,4096]{3,0,2,1:T(8,128)(2,1)}), bf16[8,16,3,4096]{3,0,2,1:T(8,128)(2,1)}, u32[]{:S(2)}, u32[]{:S(2)}) async-start(bf16[8,16,3,4096]{3,0,2,1:T(8,128)(2,1)} %copy.69), calls=%async_computation.1 | async-start | bytes 6291456 | tf_op jit(solution)/shard_map/all_to_all | solution.py:94
  110.2 13.4 %all-gather.1 = bf16[1,32,4096]{2,0,1:T(2,128)(2,1)S(1)} all-gather(bf16[1,4,4096]{2,0,1:T(2,128)(2,1)S(1)} %copy.100), channel_id=3, replica_groups=mesh['seq'=8,'expert'=16,'rep'=2] {'seq'}, dimensions={1}, use_global_device_ids=true | all-gather | bytes 294912 | tf_op jit(solution)/shard_map/all_gather | solution.py:81
  125.3 16.5 %gather_fusion.3 = bf16[384,4096]{1,0:T(8,128)(2,1)} fusion(bf16[8,4,4096]{2,1,0:T(4,128)(2,1)S(1)} %reshape.200, s32[384]{0:T(512)S(1)} %reshape.238), kind=kCustom, calls=%fused_computation.3 | custom fusion | bytes 6294528 | tf_op jit(solution)/shard_map/vmap()/gather | solution.py:29
  160.5 20.1 %all-to-all-done.1 = bf16[8,16,3,4096]{3,0,2,1:T(8,128)(2,1)} async-done(((bf16[8,16,3,4096]{3,0,2,1:T(8,128)(2,1)}), bf16[8,16,3,4096]{3,0,2,1:T(8,128)(2,1)}, u32[]{:S(2)}, u32[]{:S(2)}) %all-to-all-start.1) | async-done | bytes 3145760 | tf_op jit(solution)/shard_map/all_to_all | solution.py:94
  180.6 11.2 %all-to-all-start = ((bf16[8,16,3,4096]{3,0,2,1:T(8,128)(2,1)}), bf16[8,16,3,4096]{3,0,2,1:T(8,128)(2,1)}, u32[]{:S(2)}, u32[]{:S(2)}) async-start(bf16[8,16,3,4096]{3,0,2,1:T(8,128)(2,1)} %copy.64), calls=%async_computation | async-start | bytes 6291456 | tf_op jit(solution)/shard_map/all_to_all | solution.py:101
  192.9 11.2 %scatter_fusion.1 = s32[8,48]{1,0:T(8,128)S(1)} fusion(s32[8,48]{1,0:T(8,128)S(1)} %broadcast.147.clone, s32[256]{0:T(256)S(1)} %reshape.274, s32[256]{0:T(256)S(1)} %reshape.270), kind=kCustom, calls=%fused_computation.9 | custom fusion | bytes 5120 | tf_op jit(solution)/shard_map/vmap()/scatter | solution.py:19
  204.2 12.5 %all-gather.3 = bf16[1,32,8]{2,0,1:T(2,128)(2,1)S(1)} all-gather(bf16[1,4,8]{2,0,1:T(2,128)(2,1)S(1)} %copy.102), channel_id=5, replica_groups=mesh['seq'=8,'expert'=16,'rep'=2] {'seq'}, dimensions={1}, use_global_device_ids=true | all-gather | bytes 576 | tf_op jit(solution)/shard_map/all_gather | solution.py:82
  220.8 13.2 %all-gather.5 = bf16[1,32,4096]{2,0,1:T(2,128)(2,1)S(1)} all-gather(bf16[1,4,4096]{2,0,1:T(2,128)(2,1)S(1)} %copy.104), channel_id=7, replica_groups=mesh['seq'=8,'expert'=16,'rep'=2] {'seq'}, dimensions={1}, use_global_device_ids=true | all-gather | bytes 294912 | tf_op jit(solution)/shard_map/all_gather | solution.py:80
  235.6 16.6 %gather_fusion.7 = bf16[384,4096]{1,0:T(8,128)(2,1)} fusion(bf16[8,4,4096]{2,1,0:T(4,128)(2,1)S(1)} %reshape.208, s32[384]{0:T(512)S(1)} %reshape.256), kind=kCustom, calls=%fused_computation.7 | custom fusion | bytes 6294528 | tf_op jit(solution)/shard_map/vmap()/gather | solution.py:27
  268.1 9.3 %all-to-all-start.4 = ((bf16[8,16,3,4096]{3,0,2,1:T(8,128)(2,1)}), bf16[8,16,3,4096]{3,0,2,1:T(8,128)(2,1)}, u32[]{:S(2)}, u32[]{:S(2)}) async-start(bf16[8,16,3,4096]{3,0,2,1:T(8,128)(2,1)} %copy.86), calls=%async_computation.5 | async-start | bytes 6291456 | tf_op jit(solution)/shard_map/all_to_all | solution.py:94
  277.6 13.4 %all-gather.4 = bf16[1,32,4096]{2,0,1:T(2,128)(2,1)S(1)} all-gather(bf16[1,4,4096]{2,0,1:T(2,128)(2,1)S(1)} %copy.103), channel_id=6, replica_groups=mesh['seq'=8,'expert'=16,'rep'=2] {'seq'}, dimensions={1}, use_global_device_ids=true | all-gather | bytes 294912 | tf_op jit(solution)/shard_map/all_gather | solution.py:81
  292.8 16.5 %gather_fusion.6 = bf16[384,4096]{1,0:T(8,128)(2,1)} fusion(bf16[8,4,4096]{2,1,0:T(4,128)(2,1)S(1)} %reshape.206, s32[384]{0:T(512)S(1)} %reshape.256), kind=kCustom, calls=%fused_computation.6 | custom fusion | bytes 6294528 | tf_op jit(solution)/shard_map/vmap()/gather | solution.py:29
  327.7 20.3 %all-to-all-done.4 = bf16[8,16,3,4096]{3,0,2,1:T(8,128)(2,1)} async-done(((bf16[8,16,3,4096]{3,0,2,1:T(8,128)(2,1)}), bf16[8,16,3,4096]{3,0,2,1:T(8,128)(2,1)}, u32[]{:S(2)}, u32[]{:S(2)}) %all-to-all-start.4) | async-done | bytes 3145760 | tf_op jit(solution)/shard_map/all_to_all | solution.py:94
  348.1 11.6 %all-to-all-start.3 = ((bf16[8,16,3,4096]{3,0,2,1:T(8,128)(2,1)}), bf16[8,16,3,4096]{3,0,2,1:T(8,128)(2,1)}, u32[]{:S(2)}, u32[]{:S(2)}) async-start(bf16[8,16,3,4096]{3,0,2,1:T(8,128)(2,1)} %copy.81), calls=%async_computation.4 | async-start | bytes 6291456 | tf_op jit(solution)/shard_map/all_to_all | solution.py:101
  412.3 20.7 %all-to-all-done.3 = bf16[8,16,3,4096]{3,0,2,1:T(8,128)(2,1)} async-done(((bf16[8,16,3,4096]{3,0,2,1:T(8,128)(2,1)}), bf16[8,16,3,4096]{3,0,2,1:T(8,128)(2,1)}, u32[]{:S(2)}, u32[]{:S(2)}) %all-to-all-start.3) | async-done | bytes 3145760 | tf_op jit(solution)/shard_map/all_to_all | solution.py:101
  481.0 30.9 %all-to-all-done.2 = bf16[8,16,3,4096]{3,0,2,1:T(8,128)(2,1)} async-done(((bf16[8,16,3,4096]{3,0,2,1:T(8,128)(2,1)}), bf16[8,16,3,4096]{3,0,2,1:T(8,128)(2,1)}, u32[]{:S(2)}, u32[]{:S(2)}) %all-to-all-start.2) | async-done | bytes 3145760 | tf_op jit(solution)/shard_map/all_to_all | solution.py:118
  535.6 80.7 %all_to_all.30 = bf16[8,16,3,4096]{3,0,2,1:T(8,128)(2,1)S(1)} all-to-all(bf16[8,16,3,4096]{3,0,2,1:T(8,128)(2,1)S(1)} %copy.88), channel_id=1, replica_groups=mesh['seq'=8,'expert'=16,'rep'=2] {'expert'}, dimensions={1} | all-to-all | bytes 6291456 | tf_op jit(solution)/shard_map/all_to_all | solution.py:118
  637.2 16.4 %reduce-scatter.5.cloned.1.call-done = bf16[1,16,3,4096]{3,1,2,0:T(8,128)(2,1)} async-done(((bf16[8,16,3,4096]{3,1,2,0:T(8,128)(2,1)}), bf16[1,16,3,4096]{3,1,2,0:T(8,128)(2,1)}) %reduce-scatter.5.cloned.1.call-update) | async-done | bytes 393232 | tf_op jit(solution)/shard_map/reduce_scatter | solution.py:125
  662.6 100.8 %all-reduce.3.cloned.1.call-done = (bf16[1,192,4096]{2,1,0:T(8,128)(2,1)}, bf16[1,192,4096]{2,1,0:T(8,128)(2,1)}, bf16[1,192,4096]{2,1,0:T(8,128)(2,1)}) async-done(((bf16[1,192,4096]{2,1,0:T(8,128)(2,1)}, bf16[1,192,4096]{2,1,0:T(8,128)(2,1)}, bf16[1,192,4096]{2,1,0:T(8,128)(2,1)}), (bf16[1,192,4096]{2,1,0:T(8,128)(2,1)}, bf16[1,192,4096]{2,1,0:T(8,128)(2,1)}, ...) | async-done | bytes 4718608 | tf_op jit(solution)/shard_map/psum | solution.py:139
  (180 shorter events, 247.0 us)
Async XLA Ops:
  8.0 384.2 %copy-start = (bf16[1,192,4096]{2,1,0:T(8,128)(2,1)S(1)}, bf16[1,192,4096]{2,1,0:T(8,128)(2,1)}, u32[]{:S(2)}) copy-start(bf16[1,192,4096]{2,1,0:T(8,128)(2,1)} %param.12) | copy-start | bytes 4718596
  26.1 11.3 %copy-start.17 = (bf16[2,4,8]{2,1,0:T(4,128)(2,1)S(1)}, bf16[2,4,8]{2,1,0:T(4,128)(2,1)}, u32[]{:S(2)}) copy-start(bf16[2,4,8]{2,1,0:T(4,128)(2,1)} %param.10) | copy-start | bytes 388
  26.1 26.5 %copy-start.14 = (bf16[2,4,4096]{2,1,0:T(4,128)(2,1)S(1)}, bf16[2,4,4096]{2,1,0:T(4,128)(2,1)}, u32[]{:S(2)}) copy-start(bf16[2,4,4096]{2,1,0:T(4,128)(2,1)} %param.7) | copy-start | bytes 196612
  100.3 9.8 %copy-start.15 = (bf16[2,4,4096]{2,1,0:T(4,128)(2,1)S(1)}, bf16[2,4,4096]{2,1,0:T(4,128)(2,1)}, u32[]{:S(2)}) copy-start(bf16[2,4,4096]{2,1,0:T(4,128)(2,1)} %param.8) | copy-start | bytes 196612
  100.3 80.3 %all-to-all-start.1 = ((bf16[8,16,3,4096]{3,0,2,1:T(8,128)(2,1)}), bf16[8,16,3,4096]{3,0,2,1:T(8,128)(2,1)}, u32[]{:S(2)}, u32[]{:S(2)}) async-start(bf16[8,16,3,4096]{3,0,2,1:T(8,128)(2,1)} %copy.69), calls=%async_computation.1 | async-start | bytes 6291456 | tf_op jit(solution)/shard_map/all_to_all | solution.py:94
  180.6 87.6 %all-to-all-start = ((bf16[8,16,3,4096]{3,0,2,1:T(8,128)(2,1)}), bf16[8,16,3,4096]{3,0,2,1:T(8,128)(2,1)}, u32[]{:S(2)}, u32[]{:S(2)}) async-start(bf16[8,16,3,4096]{3,0,2,1:T(8,128)(2,1)} %copy.64), calls=%async_computation | async-start | bytes 6291456 | tf_op jit(solution)/shard_map/all_to_all | solution.py:101
  268.1 79.9 %all-to-all-start.4 = ((bf16[8,16,3,4096]{3,0,2,1:T(8,128)(2,1)}), bf16[8,16,3,4096]{3,0,2,1:T(8,128)(2,1)}, u32[]{:S(2)}, u32[]{:S(2)}) async-start(bf16[8,16,3,4096]{3,0,2,1:T(8,128)(2,1)} %copy.86), calls=%async_computation.5 | async-start | bytes 6291456 | tf_op jit(solution)/shard_map/all_to_all | solution.py:94
  348.1 85.0 %all-to-all-start.3 = ((bf16[8,16,3,4096]{3,0,2,1:T(8,128)(2,1)}), bf16[8,16,3,4096]{3,0,2,1:T(8,128)(2,1)}, u32[]{:S(2)}, u32[]{:S(2)}) async-start(bf16[8,16,3,4096]{3,0,2,1:T(8,128)(2,1)} %copy.81), calls=%async_computation.4 | async-start | bytes 6291456 | tf_op jit(solution)/shard_map/all_to_all | solution.py:101
  380.2 7.5 copy-start.5
  387.7 3.2 copy-start.6
  387.7 3.3 copy-start.18
  391.0 1.9 copy-start.1
  433.0 78.8 %all-to-all-start.2 = ((bf16[8,16,3,4096]{3,0,2,1:T(8,128)(2,1)}), bf16[8,16,3,4096]{3,0,2,1:T(8,128)(2,1)}, u32[]{:S(2)}, u32[]{:S(2)}) async-start(bf16[8,16,3,4096]{3,0,2,1:T(8,128)(2,1)} %copy.71), calls=%async_computation.2 | async-start | bytes 6291456 | tf_op jit(solution)/shard_map/all_to_all | solution.py:118
  441.5 194.0 %reduce-scatter.3.cloned.1.call-start = ((), (), s32[]{:S(2)}) async-start(), calls=%async_computation.8 | async-start | bytes 3538944 | tf_op jit(solution)/shard_map/reduce_scatter | solution.py:125
  469.5 3.2 copy-start.7
  469.5 3.3 copy-start.19
  472.8 1.9 copy-start.3
  517.1 136.5 %reduce-scatter.5.cloned.1.call-start = ((), (), s32[]{:S(2)}) async-start(), calls=%async_computation.9 | async-start | bytes 3538944 | tf_op jit(solution)/shard_map/reduce_scatter | solution.py:125
  619.7 143.7 %all-reduce.3.cloned.1.call-start = ((), (), s32[]{:S(2)}) async-start(), calls=%async_computation.10 | async-start | bytes 9437184 | tf_op jit(solution)/shard_map/psum | solution.py:139
  620.7 5.5 copy-start.2
  626.2 1.9 copy-start.4
  628.4 2.7 copy-start.12
  763.5 2.9 copy-start.10
  763.5 4.0 copy-start.9
  (6 other events, 5.6 us)
Sparse Core Ops, SparseCore 0:
  517.2 37.4 reduce-scatter.2
  619.8 33.7 reduce-scatter.4
Sparse Core Ops, SparseCore 1:
  633.9 129.5 all-reduce.2
where the time goes:
time: 782 us; the launch traced here: 776 us
  local copies, waits for them, and re-layouts  259 us (33%)
  waiting for transfers between devices  209 us (27%)
  blocking collectives  174 us (22%)
  starting transfers between devices  50.4 us (6%)
  matrix products  36.4 us (5%)
  other arithmetic  30.9 us (4%)
  between operations  16.2 us (2%)
    psum x1, waiting for transfers between devices, body(): lax.psum(total_gate.astype(jnp.bfloat16), 'rep').astype(jnp.float32)  101 us
    all_to_all x1, blocking collectives, body(): lax.all_to_all(pieces.reshape(seq_count, experts, capacity, width), 'expe...  80.7 us
    gather x4, local copies, waits for them, and re-layouts, fill_slots(): rows_in[token_at]  48.1 us
    all_to_all x2, waiting for transfers between devices, body(): lax.all_to_all(in_send.reshape(seq_count, experts, capacity, width), 'exp...  40.4 us
    gather x4, local copies, waits for them, and re-layouts, fill_slots(): rows_grad[token_at].astype(jnp.float32)  33.2 us
    all_to_all x1, waiting for transfers between devices, body(): lax.all_to_all(pieces.reshape(seq_count, experts, capacity, width), 'expe...  30.9 us
    all_gather x2, blocking collectives, body(): lax.all_gather(grad_out[micro], 'seq', axis=0, tiled=True)  26.8 us
    all_gather x2, blocking collectives, body(): lax.all_gather(tokens[micro], 'seq', axis=0, tiled=True)  26.6 us
  transfers between devices with their start and end apart: 8, of which 6 were waited for; matrix products, arithmetic and copies ran while one was open for 33% of the time, Pallas kernels for 0%

commit v1 on v0

v1 whole, which is shorter than its diff:
```python
import functools
import heapq

import jax
import jax.numpy as jnp
from jax import lax
from jax.experimental import pallas as pl
from jax.experimental.pallas import tpu as pltpu
from jax.sharding import PartitionSpec as P

MESH = pl.DeviceIdType.MESH
LANES = 128
ALL = ("seq", "expert", "rep")

ORDERS = ((0, 1, 2), (1, 2, 0), (2, 0, 1))


def gather_events(dims, unit):
    link, ready, arrived, count = {}, [], [], 0
    left = {}

    def steps(n, phase, direction):
        if n == 2:
            return 1 if direction == 1 else 0
        half = n // 2
        return half if phase > 0 or direction == 1 else half - 1

    def size(stream, phase, step):
        order = ORDERS[stream]
        blocks = 1
        for axis in order[:phase]:
            blocks *= dims[axis]
        n = dims[order[phase]]
        return blocks / 2 if (phase > 0 and n > 2 and step == n // 2) else blocks

    def begin(now, stream, phase):
        nonlocal count
        n = dims[ORDERS[stream][phase]]
        left[stream, phase] = sum(steps(n, phase, d) for d in (1, -1))
        for d in (1, -1):
            if steps(n, phase, d):
                heapq.heappush(ready, (now, count, stream, phase, d, 1))
                count += 1

    for stream in range(3):
        begin(0.0, stream, 0)
    pending = []
    while ready or pending:
        if ready and (not pending or ready[0][0] <= pending[0][0]):
            now, _, stream, phase, d, step = heapq.heappop(ready)
            axis = ORDERS[stream][phase]
            start = max(now, link.get((axis, d), 0.0))
            end = start + size(stream, phase, step) * unit
            link[axis, d] = end
            heapq.heappush(pending, (end + 1.0, count, stream, phase, d, step))
            count += 1
        else:
            now, _, stream, phase, d, step = heapq.heappop(pending)
            arrived.append((stream, phase, d, step))
            n = dims[ORDERS[stream][phase]]
            if step < steps(n, phase, d):
                heapq.heappush(ready, (now, count, stream, phase, d, step + 1))
                count += 1
            left[stream, phase] -= 1
            if left[stream, phase] == 0 and phase < 2:
                begin(now, stream, phase + 1)
    return arrived, steps, link


def gather_kernel(dims, l_ref, g_ref, got, both, send, recv, sib_send, sib_recv, pair_send, pair_recv, local):
    columns = l_ref.shape[1] // 3
    seq, expert, rep = lax.axis_index("seq"), lax.axis_index("expert"), lax.axis_index("rep")
    core = lax.rem(seq, 2)
    place = (2 * (expert // dims[2]) + rep, seq // 2, lax.rem(expert, dims[2]))

    def device(at, which):
        x, y, z = at
        return {"seq": 2 * y + which, "expert": (x // 2) * dims[2] + z, "rep": lax.rem(x, 2)}

    def neighbour(axis, d):
        at = list(place)
        at[axis] = lax.rem(at[axis] + d + dims[axis], dims[axis])
        return device(at, core)

    sibling = device(place, 1 - core)
    near = [sibling] + [neighbour(axis, d) for axis in range(3) for d in ((1, -1) if dims[axis] > 2 else (1,))]
    barrier = pltpu.get_barrier_semaphore()
    for other in near:
        pl.semaphore_signal(barrier, inc=1, device_id=other, device_id_type=MESH)
    pl.semaphore_wait(barrier, len(near))

    pair = pltpu.make_async_remote_copy(
        src_ref=l_ref, dst_ref=got, send_sem=pair_send, recv_sem=pair_recv, device_id=sibling, device_id_type=MESH)
    pair.start()
    pair.wait()
    mine, other = l_ref[...].astype(jnp.float32), got[...].astype(jnp.float32)
    first = jnp.where(core == 0, mine, other)
    second = jnp.where(core == 0, other, mine)
    half = l_ref.shape[0] // 2
    both[0] = jnp.concatenate([first[:half], second[:half]], axis=0).astype(jnp.bfloat16)
    both[1] = jnp.concatenate([first[half:], second[half:]], axis=0).astype(jnp.bfloat16)
    x, y, z = place
    own = pltpu.make_async_copy(both, g_ref.at[:, x, y, z], local)
    own.start()
    own.wait()

    def chunk(which, stream, phase, index, part):
        order = ORDERS[stream]
        at = [None] * 3
        for position, axis in enumerate(order):
            if position < phase:
                at[axis] = slice(None)
            elif position == phase:
                at[axis] = index
            else:
                at[axis] = place[axis]
        if part is not None:
            n = dims[order[0]]
            at[order[0]] = pl.ds(part * (n // 2), n // 2)
        return g_ref.at[which, at[0], at[1], at[2], :, pl.ds(stream * columns, columns)]

    arrived, steps, _ = gather_events(dims, 0.9)
    number = {event: i for i, event in enumerate(arrived)}

    def part_of(event):
        stream, phase, d, step = event
        n = dims[ORDERS[stream][phase]]
        if phase == 0 or n == 2 or step < n // 2:
            return None
        return 0 if d == 1 else 1

    def ring(event, incoming):
        stream, phase, d, step = event
        axis = ORDERS[stream][phase]
        n = dims[axis]
        index = lax.rem(place[axis] - d * (step if incoming else step - 1) + n, n)
        ref = chunk(core, stream, phase, index, part_of(event))
        i = number[event]
        return pltpu.make_async_remote_copy(
            src_ref=ref, dst_ref=ref, send_sem=send.at[i], recv_sem=recv.at[i],
            device_id=neighbour(axis, d), device_id_type=MESH)

    def across(event, incoming):
        stream, phase, d, step = event
        axis = ORDERS[stream][phase]
        n = dims[axis]
        index = lax.rem(place[axis] - d * step + n, n)
        ref = chunk(1 - core if incoming else core, stream, phase, index, part_of(event))
        i = number[event]
        return pltpu.make_async_remote_copy(
            src_ref=ref, dst_ref=ref, send_sem=sib_send.at[i], recv_sem=sib_recv.at[i],
            device_id=sibling, device_id_type=MESH)

    left = {}

    def begin(stream, phase):
        n = dims[ORDERS[stream][phase]]
        left[stream, phase] = 0
        for d in (1, -1):
            left[stream, phase] += steps(n, phase, d)
            if steps(n, phase, d):
                ring((stream, phase, d, 1), False).start()

    for stream in range(3):
        begin(stream, 0)
    for event in arrived:
        stream, phase, d, step = event
        ring(event, True).wait_recv()
        n = dims[ORDERS[stream][phase]]
        if step < steps(n, phase, d):
            ring((stream, phase, d, step + 1), False).start()
        left[stream, phase] -= 1
        if left[stream, phase] == 0 and phase < 2:
            begin(stream, phase + 1)
        across(event, False).start()
    for event in arrived:
        across(event, True).wait_recv()
    for event in arrived:
        ring(event, False).wait_send()
        across(event, False).wait_send()


def gather(dims, block):
    columns = block.shape[1]
    count = len(gather_events(dims, 0.9)[0])
    sems = lambda n: pltpu.SemaphoreType.DMA((n,))
    return pl.pallas_call(
        functools.partial(gather_kernel, dims),
        out_shape=jax.ShapeDtypeStruct((2,) + dims + (block.shape[0], columns), jnp.bfloat16),
        in_specs=[pl.BlockSpec(memory_space=pltpu.VMEM)],
        out_specs=pl.BlockSpec(memory_space=pl.ANY),
        scratch_shapes=[
            pltpu.VMEM(block.shape, jnp.bfloat16),
            pltpu.VMEM((2,) + block.shape, jnp.bfloat16),
            sems(count), sems(count), sems(count), sems(count),
            pltpu.SemaphoreType.DMA, pltpu.SemaphoreType.DMA, pltpu.SemaphoreType.DMA,
        ],
        compiler_params=pltpu.CompilerParams(collective_id=0, has_side_effects=True),
    )(block)


def dot(a, b, dims):
    return lax.dot_general(a, b, (dims, ((), ())), preferred_element_type=jnp.float32)


def forward_kernel(width, x_ref, dy_ref, wg_ref, wu_ref, wd_ref, d_ref, t_ref):
    rows = d_ref.shape[0]
    units = wg_ref.shape[0]
    x = x_ref[...].reshape(rows, x_ref.shape[-1])
    dy = dy_ref[...].reshape(rows, x_ref.shape[-1])[:, :width]
    coeff = x[:, width:].astype(jnp.float32)
    x = x[:, :width]
    lane = lax.broadcasted_iota(jnp.int32, coeff.shape, 1)
    c = jnp.sum(jnp.where(lane == lax.axis_index("expert"), coeff, 0.0), axis=1, keepdims=True)
    gate_pre = dot(x, wg_ref[...], ((1,), (1,)))
    up_pre = dot(x, wu_ref[...], ((1,), (1,)))
    d_hidden = c * dot(dy, wd_ref[...], ((1,), (1,)))
    sigma = 1.0 / (1.0 + jnp.exp(-gate_pre))
    active = gate_pre * sigma
    hidden = c * (active * up_pre)
    d_up = d_hidden * active
    d_gate = d_hidden * up_pre * sigma * (1.0 + gate_pre * (1.0 - sigma))
    d_ref[:, :units] = d_gate.astype(jnp.bfloat16)
    d_ref[:, units:] = d_up.astype(jnp.bfloat16)
    for i, value in enumerate((d_gate, d_up, hidden)):
        t_ref[i] = value.T.astype(jnp.bfloat16)


def forward(dims, gathered, wg, wu, wd):
    units, width = wg.shape
    x, y, z = dims
    rows = 2 * z * 16
    total = x * y * z * 16
    columns = gathered.shape[-1]
    block = lambda which: pl.BlockSpec((None, None, 2, z, 16, columns), lambda i: (which, i // (y // 2), i % (y // 2), 0, 0, 0))
    whole = pl.BlockSpec((units, width), lambda i: (0, 0), pipeline_mode=pl.Buffered(1))
    return pl.pallas_call(
        functools.partial(forward_kernel, width),
        grid=(x * y // 2,),
        out_shape=(jax.ShapeDtypeStruct((total, 2 * units), jnp.bfloat16), jax.ShapeDtypeStruct((3, units, total), jnp.bfloat16)),
        in_specs=[block(0), block(1), whole, whole, whole],
        out_specs=(pl.BlockSpec((rows, 2 * units), lambda i: (i, 0)), pl.BlockSpec((3, units, rows), lambda i: (0, 0, i))),
        compiler_params=pltpu.CompilerParams(vmem_limit_bytes=48 << 20),
    )(gathered, gathered, wg, wu, wd)


def weight_kernel(t_ref, x_ref, dy_ref, gate_ref, up_ref, down_ref):
    units, rows = t_ref.shape[1:]
    x = x_ref[...].reshape(rows, x_ref.shape[-1])
    dy = dy_ref[...].reshape(rows, x_ref.shape[-1])
    gate_ref[...] = dot(t_ref[0], x, ((1,), (0,))).astype(jnp.bfloat16)
    up_ref[...] = dot(t_ref[1], x, ((1,), (0,))).astype(jnp.bfloat16)
    down_ref[...] = dot(t_ref[2], dy, ((1,), (0,))).astype(jnp.bfloat16)


def weight_grads(dims, width, turned, gathered):
    units = turned.shape[1]
    tile = min(512, width)
    block = lambda which: pl.BlockSpec((None,) + dims + (16, tile), lambda i: (which, 0, 0, 0, 0, i))
    out = pl.BlockSpec((units, tile), lambda i: (0, i))
    return pl.pallas_call(
        weight_kernel,
        grid=(width // tile,),
        out_shape=[jax.ShapeDtypeStruct((units, width), jnp.bfloat16)] * 3,
        in_specs=[pl.BlockSpec(turned.shape, lambda i: (0, 0, 0), pipeline_mode=pl.Buffered(1)), block(0), block(1)],
        out_specs=[out] * 3,
        compiler_params=pltpu.CompilerParams(vmem_limit_bytes=48 << 20),
    )(turned, gathered, gathered)


AXES = ((2, 1), (1, 2))


def scatter_steps(dims, stream, phase, d):
    if phase == 2:
        return 1 if d == 1 else 0
    return dims[AXES[stream][phase]] // 2


def scatter_events(dims, shares, unit):
    link, ready, arrived, left = {}, [], [], {}
    count = 0

    def size(stream, phase, step):
        if phase == 2:
            return shares[stream]
        blocks = 2 * (dims[AXES[stream][1]] if phase == 0 else 1)
        return shares[stream] * blocks / (2 if step == dims[AXES[stream][phase]] // 2 else 1)

    def begin(now, stream, phase):
        nonlocal count
        left[stream, phase] = sum(1 for d in (1, -1) if scatter_steps(dims, stream, phase, d))
        for d in (1, -1):
            if scatter_steps(dims, stream, phase, d):
                heapq.heappush(ready, (now, count, stream, phase, d, scatter_steps(dims, stream, phase, d)))
                count += 1

    for stream in (0, 1):
        begin(0.0, stream, 0)
    pending = []
    while ready or pending:
        if ready and (not pending or ready[0][0] <= pending[0][0]):
            now, _, stream, phase, d, step = heapq.heappop(ready)
            axis = AXES[stream][phase] if phase < 2 else 0
            end = max(now, link.get((axis, d), 0.0)) + size(stream, phase, step) * unit
            link[axis, d] = end
            heapq.heappush(pending, (end + 2.0, count, stream, phase, d, step))
            count += 1
        else:
            now, _, stream, phase, d, step = heapq.heappop(pending)
            arrived.append((stream, phase, d, step))
            if step > 1:
                heapq.heappush(ready, (now, count, stream, phase, d, step - 1))
                count += 1
            else:
                left[stream, phase] -= 1
                if left[stream, phase] == 0 and phase < 2:
                    begin(now, stream, phase + 1)
    return arrived


def scatter_kernel(dims, shares, arrived, d_ref, wg_ref, wu_ref, out_ref, own, away, near, *rest):
    count = len(arrived)
    lands, last, (send, recv, pass_send, pass_recv, end_send, end_recv) = rest[:count], rest[count], rest[count + 1:]
    units = wg_ref.shape[0]
    half = wg_ref.shape[1] // 2
    seq, expert, rep = lax.axis_index("seq"), lax.axis_index("expert"), lax.axis_index("rep")
    core = lax.rem(seq, 2)
    place = (expert // dims[2], seq // 2, lax.rem(expert, dims[2]))
    sizes = (2, dims[1], dims[2])

    def device(at, which):
        return {"seq": 2 * at[1] + which, "expert": at[0] * dims[2] + at[2], "rep": rep}

    def neighbour(axis, d):
        at = list(place)
        at[axis] = lax.rem(at[axis] + d + sizes[axis], sizes[axis])
        return device(at, core)

    sibling = device(place, 1 - core)
    around = [sibling, neighbour(0, 1)] + [neighbour(axis, d) for axis in (1, 2) for d in (1, -1)]
    barrier = pltpu.get_barrier_semaphore()
    for other in around:
        pl.semaphore_signal(barrier, inc=1, device_id=other, device_id_type=MESH)
    pl.semaphore_wait(barrier, len(around))

    starts = (0, shares[0] * LANES)
    lanes = lambda stream: pl.ds(starts[stream], shares[stream] * LANES)
    pieces = []
    for stream in (0, 1):
        n = dims[AXES[stream][0]]
        offsets = [n // 2] + [d * k for k in range(n // 2 - 1, 0, -1) for d in (1, -1)] + [0]
        pieces += [((i + 0.5) / n, stream, offset) for i, offset in enumerate(offsets)]
    pieces = [piece[1:] for piece in sorted(pieces)]
    number = {piece: i for i, piece in enumerate(pieces)}

    def offset_index(axis, offset):
        return lax.rem(place[axis] + offset + sizes[axis], sizes[axis])

    def index(stream, offset):
        i = offset_index(AXES[stream][0], offset)
        return (slice(None), slice(None), i) if stream == 0 else (slice(None), i)

    def product(stream, offset, side, target):
        rows = d_ref[(slice(None), rep) + index(stream, offset)[1:]]
        shape = rows.shape[:-1]
        rows = rows.reshape(-1, 2 * units)
        cols = pl.ds(pl.multiple_of(side * half + starts[stream], LANES), shares[stream] * LANES)
        value = dot(rows[:, :units], wg_ref[:, cols], ((1,), (0,))) + dot(rows[:, units:], wu_ref[:, cols], ((1,), (0,)))
        target[index(stream, offset) + (Ellipsis, lanes(stream))] = value.astype(jnp.bfloat16).reshape(shape + (shares[stream] * LANES,))

    def passing(piece):
        stream, offset = piece
        at = index(stream, offset)
        at = at + (slice(None),) * (4 - len(at)) + (lanes(stream),)
        i = number[piece]
        return pltpu.make_async_remote_copy(
            src_ref=away.at[at], dst_ref=near.at[at], send_sem=pass_send.at[i], recv_sem=pass_recv.at[i],
            device_id=sibling, device_id_type=MESH)

    for piece in pieces:
        product(*piece, 1 - core, away)
        passing(piece).start()
    for piece in pieces:
        product(*piece, core, own)

    summed = set()

    def sum_piece(piece):
        if piece in summed:
            return
        summed.add(piece)
        passing(piece).wait_recv()
        at = index(*piece) + (Ellipsis, lanes(piece[0]))
        own[at] = own[at] + near[at]

    def chunk(event):
        stream, phase, d, step = event
        first, second = AXES[stream]
        at = [slice(None)] * 3
        if phase == 2:
            at = [1 - place[0], place[1], place[2]]
        else:
            at[(first, second)[phase]] = offset_index((first, second)[phase], d * step)
            if phase == 1:
                at[first] = place[first]
            if step == dims[(first, second)[phase]] // 2:
                at[0] = pl.ds(0 if d == 1 else 1, 1)
        return tuple(at)

    order = {event: i for i, event in enumerate(arrived)}

    def ring(event):
        stream, phase, d, step = event
        i = order[event]
        axis = AXES[stream][phase] if phase < 2 else 0
        return pltpu.make_async_remote_copy(
            src_ref=own.at[chunk(event) + (slice(None), lanes(stream))], dst_ref=lands[i], send_sem=send.at[i], recv_sem=recv.at[i],
            device_id=neighbour(axis, d), device_id_type=MESH)

    def begin(stream, phase):
        for d in (1, -1):
            step = scatter_steps(dims, stream, phase, d)
            if step:
                if phase == 0:
                    sum_piece((stream, step))
                ring((stream, phase, d, step)).start()

    left = {(stream, phase): (1 if phase == 2 else 2) for stream in (0, 1) for phase in (0, 1, 2)}
    for stream in (0, 1):
        begin(stream, 0)
    waiting = [piece for piece in pieces if piece not in summed]
    for event in arrived:
        stream, phase, d, step = event
        for _ in range(2):
            if waiting:
                sum_piece(waiting.pop(0))
        if phase == 0:
            sum_piece((stream, d * (step - 1)))
        ring(event).wait_recv()
        i = order[event]
        if phase == 2:
            at = (place[0], place[1], place[2])
        elif step == dims[AXES[stream][phase]] // 2:
            at = list(chunk((stream, phase, d, step - 1)))
            at[0] = pl.ds(0 if d == 1 else 1, 1)
            at = tuple(at)
        else:
            at = chunk((stream, phase, d, step - 1))
        at = at + (Ellipsis, lanes(stream))
        own[at] = own[at] + lands[i][...]
        if step > 1:
            ring((stream, phase, d, step - 1)).start()
        else:
            left[stream, phase] -= 1
            if left[stream, phase] == 0 and phase < 2:
                begin(stream, phase + 1)

    end = pltpu.make_async_remote_copy(
        src_ref=own.at[place[0], place[1], place[2]], dst_ref=last, send_sem=end_send, recv_sem=end_recv,
        device_id=sibling, device_id_type=MESH)
    end.start()
    for piece in pieces:
        passing(piece).wait_send()
    for event in arrived:
        ring(event).wait_send()
    end.wait()
    mine = own[place[0], place[1], place[2]].astype(jnp.float32)
    other = last[...].astype(jnp.float32)
    rows = mine.shape[0] // 2
    left_half = jnp.where(core == 0, mine[:rows], other[rows:])
    right_half = jnp.where(core == 0, other[:rows], mine[rows:])
    out_ref[:, :half] = left_half.astype(jnp.bfloat16)
    out_ref[:, half:] = right_half.astype(jnp.bfloat16)


def scatter(dims, d, wg, wu):
    units, width = wg.shape
    tiles = width // 2 // LANES
    shares = (tiles * 7 // 16, tiles - tiles * 7 // 16)
    arrived = scatter_events(dims, shares, 0.086)
    lands = []
    for stream, phase, way, step in arrived:
        columns = shares[stream] * LANES
        if phase == 2:
            lands.append((16, columns))
            continue
        n = dims[AXES[stream][phase]]
        blocks = (1 if step == n // 2 else 2,)
        lands.append(blocks + ((dims[AXES[stream][1]],) if phase == 0 else ()) + (16, columns))
    half = (2,) + dims[1:] + (16, width // 2)
    sems = lambda n: pltpu.SemaphoreType.DMA((n,))
    vmem = pl.BlockSpec(memory_space=pltpu.VMEM)
    count, pieces = len(arrived), dims[1] + dims[2]
    return pl.pallas_call(
        functools.partial(scatter_kernel, dims, shares, arrived),
        out_shape=jax.ShapeDtypeStruct((8, width), jnp.bfloat16),
        in_specs=[vmem] * 3,
        out_specs=vmem,
        scratch_shapes=[pltpu.VMEM(half, jnp.bfloat16)] * 3
        + [pltpu.VMEM(shape, jnp.bfloat16) for shape in lands]
        + [pltpu.VMEM((16, width // 2), jnp.bfloat16)]
        + [sems(count), sems(count), sems(pieces), sems(pieces), pltpu.SemaphoreType.DMA, pltpu.SemaphoreType.DMA],
        compiler_params=pltpu.CompilerParams(collective_id=1, has_side_effects=True, vmem_limit_bytes=48 << 20),
    )(d.reshape((2, 2) + dims[1:] + (16, 2 * units)), wg, wu)


def body(tokens, grad_out, expert_ids, gate_weights, w_gate, w_up, w_down):
    experts = lax.axis_size("expert")
    dims = (2 * lax.axis_size("rep"), lax.axis_size("seq") // 2, experts // 2)
    micro, rows, _ = expert_ids.shape
    width = tokens.shape[2]
    local = micro * rows
    hits = expert_ids[..., None] == jnp.arange(experts, dtype=jnp.int32)
    coeff = jnp.sum(jnp.where(hits, gate_weights[..., None], 0), axis=2).astype(jnp.bfloat16).reshape(local, experts)
    first = jnp.concatenate([tokens.reshape(local, width), jnp.pad(coeff, ((0, 0), (0, LANES - experts)))], axis=1)
    second = jnp.pad(grad_out.reshape(local, width), ((0, 0), (0, LANES)))
    gathered = gather(dims, jnp.concatenate([first, second], axis=0))
    d, turned = forward(dims, gathered, w_gate[0], w_up[0], w_down[0])
    d_tokens = scatter(dims, d, w_gate[0], w_up[0])
    grads = weight_grads(dims, width, turned, gathered)
    return (d_tokens.reshape(micro, rows, width),) + tuple(g[None] for g in grads)


def solution(mesh):
    rows = P(None, ALL, None)
    weights = P("expert", "seq", None)
    return jax.shard_map(
        body,
        mesh=mesh,
        in_specs=(rows, rows, rows, rows, weights, weights, weights),
        out_specs=(rows, weights, weights, weights),
        check_vma=False,
    )
```

time: 782 us -> 218 us (0.28)
  local copies, waits for them, and re-layouts: 259 us -> 4.06 us
  Pallas kernels: 0 us -> 211 us
  waiting for transfers between devices: 209 us -> 0 us
  blocking collectives: 174 us -> 0 us
  starting transfers between devices: 50.4 us -> 0 us
  matrix products: 36.4 us -> 0 us
  other arithmetic: 30.9 us -> 1.47 us
  between operations: 16.2 us -> 0.67 us
    pallas_call x0 -> x4, Pallas kernels: none -> 211 us  [the longest x1 120 us: gather(): pl.pallas_call(functools.partial(gather_kernel, dims), out_shape=jax.Shap...]
    psum x1 -> x0, waiting for transfers between devices: 101 us -> none  [body(): lax.psum(total_gate.astype(jnp.bfloat16), 'rep').astype(jnp.float32)]
    all_gather x7 -> x0, blocking collectives: 93 us -> none  [the longest x2 26.8 us: body(): lax.all_gather(grad_out[micro], 'seq', axis=0, tiled=True)]
    all_to_all x5 -> x0, waiting for transfers between devices: 92 us -> none  [the longest x2 40.4 us: body(): lax.all_to_all(in_send.reshape(seq_count, experts, capacity, width), 'exp...]
    gather x14 -> x0, local copies, waits for them, and re-layouts: 91.5 us -> none  [the longest x4 48.1 us: fill_slots(): rows_in[token_at]]
    all_to_all x1 -> x0, blocking collectives: 80.7 us -> none  [body(): lax.all_to_all(pieces.reshape(seq_count, experts, capacity, width), 'expe...]
    reshape x12 -> x3, local copies, waits for them, and re-layouts: 56.2 us -> 2.38 us  [the longest x1 0.86 us: body(): tokens.reshape(local, width)]
    all_to_all x5 -> x0, starting transfers between devices: 50.2 us -> none  [the longest x2 22.7 us: body(): lax.all_to_all(grad_send.reshape(seq_count, experts, capacity, width), 'e...]
  transfers between devices with their start and end apart: 8 -> 0, of which waited for: 6 -> 0; matrix products, arithmetic and copies ran while one was open for 33% -> 0% of each run, Pallas kernels for 0% -> 0%
where the time goes in v1:
time: 218 us
  Pallas kernels  211 us (97%)
  local copies, waits for them, and re-layouts  4.06 us (2%)
    pallas_call x1, Pallas kernels, gather(): pl.pallas_call(functools.partial(gather_kernel, dims), out_shape=jax.Shap...  120 us
    pallas_call x1, Pallas kernels, scatter(): pl.pallas_call(functools.partial(scatter_kernel, dims, shares, arrived),...  52.5 us
    pallas_call x1, Pallas kernels, forward(): pl.pallas_call(functools.partial(forward_kernel, width), grid=(x * y // 2...  21 us
    pallas_call x1, Pallas kernels, weight_grads(): pl.pallas_call(weight_kernel, grid=(width // tile,), out_shape=[jax.Shape...  17.6 us

profile of v1, /device:TPU:1, one launch (start us, length us, event | category | flops | bytes accessed | tf_op | source)
XLA Modules:
  0.0 217.6 jit_solution(15162766501434624367)
XLA Ops:
  0.6 0.9 reshape.27
  1.5 0.8 fusion.7
  2.3 0.9 reshape.25
  3.2 0.7 fusion.4.l_ref
  3.8 0.0 copy-start
  3.8 0.0 copy-start.1
  3.8 120.4 %shard_map.102.x_ref.dy_ref = bf16[2,4,4,8,16,4224]{5,4,3,2,1,0:T(8,128)(2,1)} custom-call(bf16[16,4224]{1,0:T(8,128)(2,1)} %fusion.4.l_ref), custom_call_target="tpu_custom_call" | custom-call | tf_op jit(solution)/shard_map/pallas_call | solution.py:187
  124.2 0.0 copy-done
  124.2 0.0 copy-done.1
  124.3 21.0 %shard_map.103 = (bf16[2048,384]{1,0:T(8,128)(2,1)S(1)}, bf16[3,192,2048]{2,1,0:T(8,128)(2,1)}) custom-call(bf16[2,4,4,8,16,4224]{5,4,3,2,1,0:T(8,128)(2,1)} %shard_map.102.x_ref.dy_ref, bf16[2,4,4,8,16,4224]{5,4,3,2,1,0:T(8,128)(2,1)} %shard_map.102.x_ref.dy_ref, bf16[192,4096]{1,0:T(8,128)(2,1)S(1)} %bitcast.8, bf16[192,4096]{1,0:T(8,128)(2,1)S(1)} %bitcast.10, ...), custom_call_target="tpu_custom_call" | custom-call | tf_op jit(solution)/shard_map/pallas_call | solution.py:237
  145.2 52.5 %shard_map.104 = bf16[8,4096]{1,0:T(8,128)(2,1)S(1)} custom-call(bf16[2,2,4,8,16,384]{5,4,3,2,1,0:T(8,128)(2,1)S(1)} %bitcast.12, bf16[192,4096]{1,0:T(8,128)(2,1)S(1)} %bitcast.9, bf16[192,4096]{1,0:T(8,128)(2,1)S(1)} %bitcast.11), custom_call_target="tpu_custom_call" | custom-call | tf_op jit(solution)/shard_map/pallas_call | solution.py:495
  197.7 0.7 reshape.29
  198.4 0.0 copy-start.2
  198.4 1.7 copy-done.2
  200.0 17.6 %shard_map.105 = (bf16[192,4096]{1,0:T(8,128)(2,1)}, bf16[192,4096]{1,0:T(8,128)(2,1)}, bf16[192,4096]{1,0:T(8,128)(2,1)}) custom-call(bf16[3,192,2048]{2,1,0:T(8,128)(2,1)S(1)} %copy-done.2, bf16[2,4,4,8,16,4224]{5,4,3,2,1,0:T(8,128)(2,1)} %shard_map.102.x_ref.dy_ref, bf16[2,4,4,8,16,4224]{5,4,3,2,1,0:T(8,128)(2,1)} %shard_map.102.x_ref.dy_ref), custom_call_target="tpu_custom_call" | custom-call | tf_op jit(solution)/shard_map/pallas_call | solution.py:261
Async XLA Ops:
  3.8 120.4 %copy-start = (bf16[1,192,4096]{2,1,0:T(8,128)(2,1)S(1)}, bf16[1,192,4096]{2,1,0:T(8,128)(2,1)}, u32[]{:S(2)}) copy-start(bf16[1,192,4096]{2,1,0:T(8,128)(2,1)} %param.11) | copy-start | bytes 4718596
  3.8 120.4 %copy-start.1 = (bf16[1,192,4096]{2,1,0:T(8,128)(2,1)S(1)}, bf16[1,192,4096]{2,1,0:T(8,128)(2,1)}, u32[]{:S(2)}) copy-start(bf16[1,192,4096]{2,1,0:T(8,128)(2,1)} %param.12) | copy-start | bytes 4718596
  198.4 1.7 copy-start.2

commit v2 on v0

v2 whole, which is shorter than its diff:
```python
import functools
import heapq
import itertools

import jax
import jax.numpy as jnp
from jax import lax
from jax.experimental import pallas as pl
from jax.experimental.pallas import tpu as pltpu
from jax.sharding import PartitionSpec as P

MESH = pl.DeviceIdType.MESH
LANES = 128
ALL = ("seq", "expert", "rep")

ORDERS = ((0, 1, 2), (2, 1, 0), (2, 0, 1))
BACK = ((0, 1, 2), (0, 2, 1))


def offsets(n):
    return [0] + [d * k for k in range(1, n // 2) for d in (1, -1)] + [n // 2]


def reaches(n, turn):
    return [(d, m) for d, m in ((1, n // 2 - turn % 2), (-1, n // 2 - 1 + turn % 2)) if m]


class Plan:
    def __init__(self, dims, orders, tiles, unit=0.0862, latency=1.75):
        self.dims, self.orders, self.tiles, self.unit, self.latency = dims, orders, tiles, unit, latency
        self.arrived, self.after, self.time = [], {}, {}
        link, ready, pending, got, tick = {}, [], [], {}, itertools.count()

        def begin(now, stream, phase, piece):
            first = [(stream, phase, piece, d, 1) for d, _ in self.ways(stream, phase, piece)]
            for message in first:
                heapq.heappush(ready, (now, next(tick), message))
            return first

        self.first = [m for s in range(len(orders)) for phase in (0, 1) for m in begin(0.0, s, phase, 0)]
        while ready or pending:
            if ready and (not pending or ready[0][0] <= pending[0][0]):
                now, _, message = heapq.heappop(ready)
                heapq.heappush(pending, (self.sent(link, now, message), next(tick), message))
                continue
            now, _, message = heapq.heappop(pending)
            self.arrived.append(message)
            self.time[message] = now
            stream, phase, piece, d, hop = message
            sets_off = []
            if hop < dict(self.ways(stream, phase, piece))[d]:
                sets_off.append((stream, phase, piece, d, hop + 1))
                heapq.heappush(ready, (now, next(tick), sets_off[0]))
            off = self.offset(message)
            got[stream, phase, off] = got.get((stream, phase, off), 0) + 1
            got[stream, phase] = got.get((stream, phase), 0) + 1
            if phase == 0:
                sets_off += begin(now, stream, 1, off)
                if got[stream, 0] == self.ring(stream, 0) - 1:
                    sets_off += begin(now, stream, 2, 0)
            elif phase == 1 and got[stream, 1, off] == self.ring(stream, 0):
                sets_off += begin(now, stream, 2, off)
            self.after[message] = sets_off

    def ring(self, stream, phase):
        return self.dims[self.orders[stream][phase]]

    def ways(self, stream, phase, piece):
        turn = offsets(self.ring(stream, phase - 1)).index(piece) if phase else 0
        return reaches(self.ring(stream, phase), turn)

    def sent(self, link, now, message):
        stream, phase, _, d, _ = message
        key = self.orders[stream][phase], d
        link[key] = max(now, link.get(key, 0.0)) + self.unit * self.tiles[stream] * (self.ring(stream, 0) if phase == 2 else 1)
        return link[key] + self.latency

    def offset(self, message):
        stream, phase, _, d, hop = message
        n = self.ring(stream, phase)
        return n // 2 if 2 * hop == n else -d * hop


class Back(Plan):
    def __init__(self, *args):
        super().__init__(*args)
        messages = list(reversed(self.arrived))
        self.needs = {m: self.needed(m) for m in messages}
        self.first = [m for m in messages if not self.needs[m]]
        link, done, came = {}, set(), []
        ready = [(0.0, i, m) for i, m in enumerate(messages) if not self.needs[m]]
        rank = {m: i for i, m in enumerate(messages)}
        pending, started = [], set(self.first)
        while ready or pending:
            if ready and (not pending or ready[0][0] <= pending[0][0]):
                now, i, message = heapq.heappop(ready)
                heapq.heappush(pending, (self.sent(link, now, message), i, message))
                continue
            now, _, message = heapq.heappop(pending)
            done.add(message)
            came.append(message)
            self.time[message] = now
            self.after[message] = [m for m in messages if m not in started and self.needs[m] <= done]
            for m in self.after[message]:
                started.add(m)
                heapq.heappush(ready, (now, rank[m], m))
        self.arrived = came

    def needed(self, message):
        stream, phase, piece, d, hop = message
        off = self.offset(message)
        needs = set()
        if hop < dict(self.ways(stream, phase, piece))[d]:
            needs.add((stream, phase, piece, d, hop + 1))
        if phase < 2:
            needs |= {(stream, phase + 1, off, way, 1) for way, _ in self.ways(stream, phase + 1, off)}
        if phase == 0:
            needs |= {(stream, 2, 0, way, 1) for way, _ in self.ways(stream, 2, 0)}
        return needs


def dot(a, b, dims):
    return lax.dot_general(a, b, (dims, ((), ())), preferred_element_type=jnp.float32)


def layer_kernel(dims, plan, back, lag,
                 tok_hbm, grad_hbm, ids_hbm, gates_hbm, wg_hbm, wu_hbm, wd_hbm,
                 g_ref, out_ref, gate_hbm, up_hbm, down_hbm,
                 tok_ref, grad_ref, ids_ref, gates_ref, block, got, both, wg_ref, wu_ref, wd_ref, wcat, stage, acc, c_ref,
                 dcat, turned, tiles_ref, grads_ref, own, land, last,
                 in_sem, weight_sem, half_sem, wsend, wrecv, pair_send, pair_recv, local,
                 send, recv, sib_send, sib_recv, load_sem, dsend, drecv, bsend, brecv, tile_sem, grad_sem, end_send, end_recv):
    units, width = wg_ref.shape
    half = width // 2
    micro = tok_ref.shape[0]
    tiles = plan.tiles
    starts = [sum(tiles[:s]) * LANES for s in range(3)]
    seq, expert, rep = lax.axis_index("seq"), lax.axis_index("expert"), lax.axis_index("rep")
    core = lax.rem(seq, 2)
    place = (2 * (expert // dims[2]) + rep, seq // 2, lax.rem(expert, dims[2]))

    def many(pairs, sem):
        return [pltpu.make_async_copy(a, b, sem.at[i]) for i, (a, b) in enumerate(pairs)]

    inputs = many(((tok_hbm, tok_ref), (grad_hbm, grad_ref), (ids_hbm, ids_ref), (gates_hbm, gates_ref)), in_sem)
    weights = many(((wg_hbm, wg_ref), (wu_hbm, wu_ref), (wd_hbm, wd_ref)), weight_sem)
    mine_half = pl.ds(pl.multiple_of(core * half, LANES), half)
    other_half = pl.ds(pl.multiple_of((1 - core) * half, LANES), half)
    halves = many(((wg_hbm.at[:, mine_half], wcat.at[pl.ds(0, units)]), (wu_hbm.at[:, mine_half], wcat.at[pl.ds(units, units)])), half_sem)
    for copy in inputs:
        copy.start()

    def device(at, which):
        x, y, z = at
        return {"seq": 2 * y + which, "expert": (x // 2) * dims[2] + z, "rep": lax.rem(x, 2)}

    def shifted(axis, offset):
        return lax.rem(place[axis] + offset + dims[axis], dims[axis])

    def neighbour(axis, d):
        at = list(place)
        at[axis] = shifted(axis, d)
        return device(at, core)

    sibling = device(place, 1 - core)
    around = [sibling] + [neighbour(axis, d) for axis in range(3) for d in (1, -1)] + [neighbour(0, 2)]
    barrier = pltpu.get_barrier_semaphore()
    for other in around:
        pl.semaphore_signal(barrier, inc=1, device_id=other, device_id_type=MESH)
    for copy in inputs:
        copy.wait()

    rows_of = lambda ref: jnp.concatenate([ref[m].astype(jnp.float32) for m in range(micro)], axis=0)
    ids = jnp.concatenate([ids_ref[m] for m in range(micro)], axis=0)
    gates = rows_of(gates_ref)
    lane = lax.broadcasted_iota(jnp.int32, (ids.shape[0], LANES), 1)
    coeff = jnp.zeros(lane.shape, jnp.float32)
    for k in range(ids.shape[1]):
        coeff = coeff + jnp.where(lane == ids[:, k:k + 1], gates[:, k:k + 1], 0.0)
    block[:, :width] = jnp.concatenate([rows_of(tok_ref), rows_of(grad_ref)], axis=0).astype(jnp.bfloat16)
    block[:, width:] = jnp.concatenate([coeff, jnp.zeros_like(coeff)], axis=0).astype(jnp.bfloat16)
    pl.semaphore_wait(barrier, len(around))

    pair = pltpu.make_async_remote_copy(
        src_ref=block, dst_ref=got, send_sem=pair_send, recv_sem=pair_recv, device_id=sibling, device_id_type=MESH)
    pair.start()
    for copy in weights + halves:
        copy.start()
    pair.wait()
    mine, other = block[...].astype(jnp.float32), got[...].astype(jnp.float32)
    first = jnp.where(core == 0, mine, other)
    second = jnp.where(core == 0, other, mine)
    rows = block.shape[0] // 2
    upper = jnp.concatenate([first[:rows], second[:rows]], axis=0)
    lower = jnp.concatenate([first[rows:], second[rows:]], axis=0)
    both[...] = jnp.where(core == 0, upper, lower).astype(jnp.bfloat16)
    x, y, z = place
    copy = pltpu.make_async_copy(both, g_ref.at[core, x, y, z], local)
    copy.start()
    copy.wait()

    def chunk(which, stream, phase, piece, offset):
        a, b, c = ORDERS[stream]
        at = [None] * 3
        if phase == 0:
            at[a], at[b], at[c] = shifted(a, offset), place[b], place[c]
        elif phase == 1:
            at[a], at[b], at[c] = shifted(a, piece), shifted(b, offset), place[c]
        elif piece is None:
            at[a], at[b], at[c] = slice(None), slice(None), shifted(c, offset)
        else:
            at[a], at[b], at[c] = slice(None), shifted(b, piece), shifted(c, offset)
        return g_ref.at[which, at[0], at[1], at[2], :, pl.ds(starts[stream], tiles[stream] * LANES)]

    number = {message: i for i, message in enumerate(plan.arrived)}

    def ring(message, incoming):
        stream, phase, piece, d, hop = message
        ref = chunk(core, stream, phase, piece, -d * (hop if incoming else hop - 1))
        i = number[message]
        return pltpu.make_async_remote_copy(
            src_ref=ref, dst_ref=ref, send_sem=send.at[i], recv_sem=recv.at[i],
            device_id=neighbour(ORDERS[stream][phase], d), device_id_type=MESH)

    copies = [(s, None, 0) for s in range(3)] + [(m[0], m[2], plan.offset(m)) for m in plan.arrived if m[1] == 2]
    place_of = {copy: i for i, copy in enumerate(copies)}

    def across(copy, incoming):
        stream, piece, offset = copy
        ref = chunk(1 - core if incoming else core, stream, 2, piece, offset)
        i = place_of[copy]
        return pltpu.make_async_remote_copy(
            src_ref=ref, dst_ref=ref, send_sem=sib_send.at[i], recv_sem=sib_recv.at[i],
            device_id=sibling, device_id_type=MESH)

    due = {}
    for message in plan.arrived:
        key = message[0], (plan.offset(message) if message[1] == 2 else 0)
        due[key] = max(due.get(key, 0.0), plan.time[message])
    tasks = sorted(due, key=lambda key: due[key])

    def shape_of(stream):
        return tuple(dims[axis] for axis in sorted(ORDERS[stream][:2]))

    def fetch(task):
        stream, offset = task
        slot = tasks.index(task) % 2
        one, two = shape_of(stream)
        return [pltpu.make_async_copy(
            chunk(which, stream, 2, None, offset),
            stage.at[slot, which, pl.ds(0, one), pl.ds(0, two), :, pl.ds(0, tiles[stream] * LANES)],
            load_sem.at[slot, which]) for which in (0, 1)]

    def load(task):
        stream, offset = task
        for copy in copies:
            if copy[0] == stream and copy[2] == offset:
                across(copy, True).wait_recv()
        for copy in fetch(task):
            copy.start()

    def compute(task):
        stream, offset = task
        slot = tasks.index(task) % 2
        one, two = shape_of(stream)
        for copy in fetch(task):
            copy.wait()
        at = [slice(None)] * 3
        at[ORDERS[stream][2]] = shifted(ORDERS[stream][2], offset)
        columns = tiles[stream] * LANES
        depth = min(columns, width - starts[stream])
        part = pl.ds(starts[stream], depth)
        step = min(one, max(1, 256 // (two * 16)))

        @pl.loop(0, one // step)
        def _(i):
            some = pl.ds(i * step, step)
            x, dy = (stage[slot, which, some, pl.ds(0, two), :, pl.ds(0, columns)].reshape(-1, columns) for which in (0, 1))
            where = list(at)
            where[min(ORDERS[stream][:2])] = some
            where = tuple(where)
            for j, (rows, w) in enumerate(((x, wg_ref), (x, wu_ref), (dy, wd_ref))):
                value = dot(rows[:, :depth], w[:, part], ((1,), (1,))).reshape(step, two, 16, units)
                acc[(j,) + where] = acc[(j,) + where] + value
            if columns > depth:
                lane = lax.broadcasted_iota(jnp.int32, (step * two * 16, LANES), 1)
                picked = jnp.where(lane == expert, x[:, depth:].astype(jnp.float32), 0.0)
                c_ref[where] = jnp.sum(picked, axis=1, keepdims=True).reshape(step, two, 16, 1)

    for message in plan.first:
        ring(message, False).start()
    acc[...] = jnp.zeros_like(acc)
    for copy in weights + halves:
        copy.wait()
    lent = [pltpu.make_async_remote_copy(
        src_ref=ref.at[:, other_half], dst_ref=wcat.at[pl.ds((2 + i) * units, units)], send_sem=wsend.at[i], recv_sem=wrecv.at[i],
        device_id=sibling, device_id_type=MESH) for i, ref in enumerate((wg_ref, wu_ref))]
    for copy in lent:
        copy.start()
    left = {s: sum(1 for m in plan.arrived if m[0] == s and m[1] < 2) for s in range(3)}
    queue, loaded = list(tasks), []
    for message in plan.arrived:
        ring(message, True).wait_recv()
        for later in plan.after[message]:
            ring(later, False).start()
        stream, phase, piece, d, hop = message
        if phase < 2:
            left[stream] -= 1
            if left[stream] == 0:
                across((stream, None, 0), False).start()
        else:
            across((stream, piece, plan.offset(message)), False).start()
        if loaded:
            compute(loaded.pop())
        if queue and due[queue[0]] + lag < plan.time[message]:
            loaded.append(queue.pop(0))
            load(loaded[0])
    for task in queue:
        load(task)
        for before in loaded:
            compute(before)
        loaded = [task]
    compute(loaded[0])

    rows = 2 * dims[2] * 16

    def activate(x, y, store):
        part = lambda ref: ref[x, pl.ds(y, 2)].reshape(rows, ref.shape[-1])
        c = part(c_ref)
        gate_pre, up_pre, d_hidden = (part(acc.at[j]) for j in range(3))
        d_hidden = c * d_hidden
        sigma = jax.nn.sigmoid(gate_pre)
        active = gate_pre * sigma
        hidden = c * (active * up_pre)
        d_up = d_hidden * active
        d_gate = d_hidden * up_pre * sigma * (1.0 + gate_pre * (1.0 - sigma))
        if store is not None:
            for j, value in enumerate((d_gate, d_up)):
                dcat[store, pl.ds(y, 2), :, :, j * units:(j + 1) * units] = value.astype(jnp.bfloat16).reshape(2, dims[2], 16, units)
        at = pl.ds(pl.multiple_of((x * dims[1] + y) * dims[2] * 16, rows), rows)
        for j, value in enumerate((d_gate, d_up, hidden)):
            turned[j * units:(j + 1) * units, at] = value.T.astype(jnp.bfloat16)

    def swap(i):
        return pltpu.make_async_remote_copy(
            src_ref=dcat.at[i, :, :, :, pl.ds(0, 2 * units)], dst_ref=dcat.at[i, :, :, :, pl.ds(2 * units, 2 * units)],
            send_sem=dsend.at[i], recv_sem=drecv.at[i], device_id=sibling, device_id_type=MESH)

    for i in (0, 1):
        @pl.loop(0, dims[1] // 2)
        def _(pair_of):
            activate(2 * i + rep, 2 * pair_of, i)
        swap(i).start()

    spot = (place[0] // 2, place[1], place[2])
    back_starts = (0, back.tiles[0] * LANES)
    sizes = back.dims

    def moved(axis, offset):
        return lax.rem(spot[axis] + offset + sizes[axis], sizes[axis])

    def lanes(stream):
        return pl.ds(back_starts[stream], back.tiles[stream] * LANES)

    def region(stream, phase, piece, offset):
        a, b, c = BACK[stream]
        at = [None] * 3
        if phase == 0:
            at[a], at[b], at[c] = moved(a, offset), spot[b], spot[c]
        elif phase == 1:
            at[a], at[b], at[c] = moved(a, piece), moved(b, offset), spot[c]
        else:
            at[a], at[b], at[c] = slice(None), moved(b, piece), moved(c, offset)
        return tuple(at) + (slice(None), lanes(stream))

    rank = {message: i for i, message in enumerate(back.arrived)}

    def landing(message):
        stream, phase = message[:2]
        ref = land.at[rank[message]]
        columns = pl.ds(0, back.tiles[stream] * LANES)
        return ref.at[:, :, columns] if phase == 2 else ref.at[0, :, columns]

    def hand(message):
        stream, phase, piece, d, hop = message
        i = rank[message]
        axis = BACK[stream][phase]
        return pltpu.make_async_remote_copy(
            src_ref=own.at[region(stream, phase, piece, -d * hop)], dst_ref=landing(message), send_sem=bsend.at[i], recv_sem=brecv.at[i],
            device_id=neighbour(axis, -2 * d if axis == 0 else -d), device_id_type=MESH)

    made = set()

    def make(stream, offset):
        if (stream, offset) in made:
            return
        made.add((stream, offset))
        c = BACK[stream][2]
        at = (slice(None), slice(None), moved(c, offset)) if c == 2 else (slice(None), moved(c, offset))
        part = dcat[at]
        columns = back.tiles[stream] * LANES
        value = dot(part.reshape(-1, 4 * units), wcat[:, lanes(stream)], ((1,), (0,)))
        own[at + (Ellipsis, lanes(stream))] = value.astype(jnp.bfloat16).reshape(part.shape[:-1] + (columns,))

    def source(message):
        return message[0], (back.offset(message) if message[1] == 2 else 0)

    def target(message):
        stream, phase, piece, d, hop = message
        return stream, (-d * (hop - 1) if phase == 2 else 0)

    width_of = tiles_ref.shape[-1]
    count = width // width_of
    total = turned.shape[1]

    def tile(i):
        cols = pl.ds(i * width_of, width_of)
        return [pltpu.make_async_copy(g_ref.at[which, :, :, :, :, cols], tiles_ref.at[i % 2, which], tile_sem.at[i % 2, which]) for which in (0, 1)]

    def result(i):
        cols = pl.ds(i * width_of, width_of)
        return [pltpu.make_async_copy(grads_ref.at[i % 2, pl.ds(j * units, units)], ref.at[:, cols], grad_sem.at[i % 2, j])
                for j, ref in enumerate((gate_hbm, up_hbm, down_hbm))]

    def weigh(i):
        if i + 1 < count:
            for copy in tile(i + 1):
                copy.start()
        for copy in tile(i):
            copy.wait()
        if i >= 2:
            for copy in result(i - 2):
                copy.wait()
        x, dy = (tiles_ref[i % 2, which].reshape(total, width_of) for which in (0, 1))
        grads_ref[i % 2, :2 * units] = dot(turned[:2 * units], x, ((1,), (0,))).astype(jnp.bfloat16)
        grads_ref[i % 2, 2 * units:] = dot(turned[2 * units:], dy, ((1,), (0,))).astype(jnp.bfloat16)
        for copy in result(i):
            copy.start()

    for copy in tile(0):
        copy.start()
    for copy in lent:
        copy.wait()
    for i in (0, 1):
        swap(i).wait_recv()
    for message in back.first:
        make(*source(message))
        hand(message).start()
    fill = [functools.partial(activate, 2 * i + 1 - rep, y, None) for i in (0, 1) for y in range(0, dims[1], 2)]
    fill += [functools.partial(weigh, i) for i in range(count)]
    fills, filled = len(fill), 0
    rest = [(s, o) for s, _ in enumerate(BACK) for o in offsets(sizes[BACK[s][2]])]
    for number_of, message in enumerate(back.arrived):
        make(*target(message))
        for later in back.after[message]:
            make(*source(later))
        while filled < fills and filled * (len(back.arrived) - 6) < fills * number_of:
            fill[filled]()
            filled += 1
        hand(message).wait_recv()
        stream, phase, piece, d, hop = message
        at = region(stream, phase, piece, -d * (hop - 1))
        own[at] = own[at] + landing(message)[...]
        for later in back.after[message]:
            hand(later).start()

    end = pltpu.make_async_remote_copy(
        src_ref=own.at[spot], dst_ref=last, send_sem=end_send, recv_sem=end_recv, device_id=sibling, device_id_type=MESH)
    end.start()
    while filled < fills:
        fill[filled]()
        filled += 1
    for copy in copies:
        across(copy, False).wait_send()
    for message in plan.arrived:
        ring(message, False).wait_send()
    for message in back.arrived:
        hand(message).wait_send()
    for i in (0, 1):
        swap(i).wait_send()
    end.wait()
    mine = own[spot].astype(jnp.float32)
    other = last[...].astype(jnp.float32)
    rows = mine.shape[0] // 2
    left_half = jnp.where(core == 0, mine[:rows], other[rows:])
    right_half = jnp.where(core == 0, other[:rows], mine[rows:])
    each = out_ref.shape[1]
    for m in range(micro):
        out_ref[m, :, :half] = left_half[m * each:(m + 1) * each].astype(jnp.bfloat16)
        out_ref[m, :, half:] = right_half[m * each:(m + 1) * each].astype(jnp.bfloat16)
    for i in range(max(0, count - 2), count):
        for copy in result(i):
            copy.wait()


def layer(dims, tokens, grad_out, ids, gates, wg, wu, wd):
    units, width = wg.shape
    columns = width + LANES
    half = width // 2
    n = columns // LANES
    tiles = (n // 3, n // 3, n - 2 * (n // 3))
    plan = Plan(dims, ORDERS, tiles)
    narrow = half // LANES * 7 // 16
    back = Back((2,) + dims[1:], BACK, (narrow, half // LANES - narrow))
    count, back_count = len(plan.arrived), len(back.arrived)
    local = 2 * tokens.shape[0] * tokens.shape[1]
    total = dims[0] * dims[1] * dims[2] * 16
    tile = min(256, width)
    bf16 = lambda *shape: pltpu.VMEM(shape, jnp.bfloat16)
    like = lambda a: pltpu.VMEM(a.shape, a.dtype)
    sems = lambda *n: pltpu.SemaphoreType.DMA(n)
    one = pltpu.SemaphoreType.DMA
    vmem, hbm = pl.BlockSpec(memory_space=pltpu.VMEM), pl.BlockSpec(memory_space=pl.ANY)
    grad = jax.ShapeDtypeStruct((units, width), jnp.bfloat16)
    return pl.pallas_call(
        functools.partial(layer_kernel, dims, plan, back, 4.0),
        out_shape=(
            jax.ShapeDtypeStruct((2,) + dims + (16, columns), jnp.bfloat16),
            jax.ShapeDtypeStruct(tokens.shape, jnp.bfloat16),
            grad, grad, grad,
        ),
        in_specs=[hbm] * 7,
        out_specs=(hbm, vmem, hbm, hbm, hbm),
        scratch_shapes=[
            like(tokens), like(grad_out), like(ids), like(gates),
            bf16(local, columns), bf16(local, columns), bf16(local, columns),
            bf16(units, width), bf16(units, width), bf16(units, width),
            bf16(4 * units, half),
            bf16(2, 2, max(dims[0], dims[1]), max(dims[1], dims[2]), 16, max(tiles) * LANES),
            pltpu.VMEM((3,) + dims + (16, units), jnp.float32),
            pltpu.VMEM(dims + (16, 1), jnp.float32),
            bf16(2, dims[1], dims[2], 16, 4 * units),
            bf16(3 * units, total),
            bf16(2, 2, *dims, 16, tile),
            bf16(2, 3 * units, tile),
            bf16(2, dims[1], dims[2], 16, half),
            bf16(back_count, 2, 16, max(back.tiles) * LANES),
            bf16(16, half),
            sems(4), sems(3), sems(2), sems(2), sems(2), one, one, one,
            sems(count), sems(count), sems(count), sems(count), sems(2, 2),
            sems(2), sems(2), sems(back_count), sems(back_count), sems(2, 2), sems(2, 3), one, one,
        ],
        compiler_params=pltpu.CompilerParams(collective_id=0, has_side_effects=True, vmem_limit_bytes=60 << 20),
    )(tokens, grad_out, ids, gates, wg, wu, wd)


def body(tokens, grad_out, expert_ids, gate_weights, w_gate, w_up, w_down):
    dims = (2 * lax.axis_size("rep"), lax.axis_size("seq") // 2, lax.axis_size("expert") // 2)
    _, d_tokens, *grads = layer(dims, tokens, grad_out, expert_ids, gate_weights, w_gate[0], w_up[0], w_down[0])
    return (d_tokens,) + tuple(g[None] for g in grads)


def solution(mesh):
    rows = P(None, ALL, None)
    weights = P("expert", "seq", None)
    return jax.shard_map(
        body,
        mesh=mesh,
        in_specs=(rows, rows, rows, rows, weights, weights, weights),
        out_specs=(rows, weights, weights, weights),
        check_vma=False,
    )
```

time: 782 us -> 164 us (0.21)
  local copies, waits for them, and re-layouts: 259 us -> 7.43 us
  waiting for transfers between devices: 209 us -> 0 us
  blocking collectives: 174 us -> 0 us
  Pallas kernels: 0 us -> 155 us
  starting transfers between devices: 50.4 us -> 0 us
  matrix products: 36.4 us -> 0 us
  other arithmetic: 30.9 us -> 0 us
  between operations: 16.2 us -> 0.65 us
    pallas_call x0 -> x1, Pallas kernels: none -> 155 us  [layer(): pl.pallas_call(functools.partial(layer_kernel, dims, plan, back, 4.0), ou...]
    psum x1 -> x0, waiting for transfers between devices: 101 us -> none  [body(): lax.psum(total_gate.astype(jnp.bfloat16), 'rep').astype(jnp.float32)]
    all_gather x7 -> x0, blocking collectives: 93 us -> none  [the longest x2 26.8 us: body(): lax.all_gather(grad_out[micro], 'seq', axis=0, tiled=True)]
    all_to_all x5 -> x0, waiting for transfers between devices: 92 us -> none  [the longest x2 40.4 us: body(): lax.all_to_all(in_send.reshape(seq_count, experts, capacity, width), 'exp...]
    gather x14 -> x0, local copies, waits for them, and re-layouts: 91.5 us -> none  [the longest x4 48.1 us: fill_slots(): rows_in[token_at]]
    all_to_all x1 -> x0, blocking collectives: 80.7 us -> none  [body(): lax.all_to_all(pieces.reshape(seq_count, experts, capacity, width), 'expe...]
    reshape x12 -> x0, local copies, waits for them, and re-layouts: 56.2 us -> none  [the longest x4 25.9 us: body(): pieces.reshape(seq_count, experts, capacity, width)]
    all_to_all x5 -> x0, starting transfers between devices: 50.2 us -> none  [the longest x2 22.7 us: body(): lax.all_to_all(grad_send.reshape(seq_count, experts, capacity, width), 'e...]
  transfers between devices with their start and end apart: 8 -> 0, of which waited for: 6 -> 0; matrix products, arithmetic and copies ran while one was open for 33% -> 0% of each run, Pallas kernels for 0% -> 0%
where the time goes in v2:
time: 164 us; the launch traced here: 163 us
  Pallas kernels  155 us (95%)
  local copies, waits for them, and re-layouts  7.43 us (5%)
    pallas_call x1, Pallas kernels, layer(): pl.pallas_call(functools.partial(layer_kernel, dims, plan, back, 4.0), ou...  155 us
    unnamed x8, local copies, waits for them, and re-layouts  7.43 us

profile of v2, /device:TPU:1, one launch (start us, length us, event | category | flops | bytes accessed | tf_op | source)
XLA Modules:
  0.0 163.0 jit_solution(3200090940952737889)
XLA Ops:
  0.6 154.9 %shard_map.102 = (bf16[2,4,4,8,16,4224]{5,4,3,2,1,0:T(8,128)(2,1)}, bf16[2,4,4096]{2,1,0:T(4,128)(2,1)}, bf16[192,4096]{1,0:T(8,128)(2,1)}, bf16[192,4096]{1,0:T(8,128)(2,1)}, bf16[192,4096]{1,0:T(8,128)(2,1)}) custom-call(bf16[2,4,4096]{2,1,0:T(4,128)(2,1)} %tok_hbm.1, bf16[2,4,4096]{2,1,0:T(4,128)(2,1)} %grad_hbm.1, s32[2,4,8]{2,1,0:T(4,128)} %ids_hbm.1, ...), custom_call_target="tpu_custom_call" | custom-call | tf_op jit(solution)/shard_map/pallas_call | solution.py:515
  155.5 1.5 copy.15
  157.0 0.0 copy-start.1
  157.0 2.8 %copy.16 = bf16[1,192,4096]{2,1,0:T(8,128)(2,1)} copy(bf16[1,192,4096]{2,1,0:T(8,128)(2,1)} %bitcast.11) | data formatting | bytes 3145728
  159.8 0.0 copy-done.1
  159.8 0.0 copy-start
  159.9 1.1 copy.17
  161.0 0.8 copy-done
  161.8 1.1 copy.18
Async XLA Ops:
  157.0 2.8 %copy-start.1 = (bf16[192,4096]{1,0:T(8,128)(2,1)S(1)}, bf16[192,4096]{1,0:T(8,128)(2,1)}, u32[]{:S(2)}) copy-start(bf16[192,4096]{1,0:T(8,128)(2,1)} %get-tuple-element.10) | copy-start | bytes 4718596
  159.8 2.0 %copy-start = (bf16[192,4096]{1,0:T(8,128)(2,1)S(1)}, bf16[192,4096]{1,0:T(8,128)(2,1)}, u32[]{:S(2)}) copy-start(bf16[192,4096]{1,0:T(8,128)(2,1)} %get-tuple-element.11) | copy-start | bytes 4718596

commit v3 on v2

v3 whole, which is shorter than its diff:
```python
import functools
import heapq
import itertools

import jax
import jax.numpy as jnp
from jax import lax
from jax.experimental import pallas as pl
from jax.experimental.pallas import tpu as pltpu
from jax.sharding import PartitionSpec as P

MESH = pl.DeviceIdType.MESH
LANES = 128
ALL = ("seq", "expert", "rep")

ORDERS = ((0, 1, 2), (0, 2, 1), (0, 2, 1))
BACK = ((0, 1, 2), (0, 2, 1))


def offsets(n):
    return [0] + [d * k for k in range(1, n // 2) for d in (1, -1)] + [n // 2]


def reaches(n, turn):
    return [(d, m) for d, m in ((1, n // 2 - turn % 2), (-1, n // 2 - 1 + turn % 2)) if m]


class Plan:
    def __init__(self, dims, orders, tiles, starts=(0.0, 0.0, 0.0), unit=0.0862, latency=1.75):
        self.dims, self.orders, self.tiles, self.unit, self.latency = dims, orders, tiles, unit, latency
        self.arrived, self.after, self.time, self.whole = [], {}, {}, {}
        link, ready, pending, got, tick = {}, [], [], {}, itertools.count()

        def begin(now, stream, phase, piece):
            first = [(stream, phase, piece, d, 1) for d, _ in self.ways(stream, phase, piece)]
            for message in first:
                heapq.heappush(ready, (now, next(tick), message))
            return first

        self.first = [m for s in range(len(orders)) for phase in (0, 1) for m in begin(starts[s], s, phase, 0)]
        while ready or pending:
            if ready and (not pending or ready[0][0] <= pending[0][0]):
                now, _, message = heapq.heappop(ready)
                heapq.heappush(pending, (self.sent(link, now, message), next(tick), message))
                continue
            now, _, message = heapq.heappop(pending)
            self.arrived.append(message)
            self.time[message] = now
            stream, phase, piece, d, hop = message
            sets_off, whole = [], []
            if hop < dict(self.ways(stream, phase, piece))[d]:
                sets_off.append((stream, phase, piece, d, hop + 1))
                heapq.heappush(ready, (now, next(tick), sets_off[0]))
            off = self.offset(message)
            got[stream, phase, off] = got.get((stream, phase, off), 0) + 1
            got[stream, phase] = got.get((stream, phase), 0) + 1
            if phase == 0:
                sets_off += begin(now, stream, 1, off)
                if got[stream, 0] == self.ring(stream, 0) - 1:
                    sets_off += begin(now, stream, 2, 0)
                    whole.append((stream, 0, 0))
            elif phase == 1 and got[stream, 1, off] == self.ring(stream, 0):
                sets_off += begin(now, stream, 2, off)
                whole.append((stream, off, 0))
            elif phase == 2:
                whole.append((stream, piece, off))
            self.after[message], self.whole[message] = sets_off, whole

    def ring(self, stream, phase):
        return self.dims[self.orders[stream][phase]]

    def ways(self, stream, phase, piece):
        turn = offsets(self.ring(stream, phase - 1)).index(piece) if phase else 0
        return reaches(self.ring(stream, phase), turn)

    def sent(self, link, now, message):
        stream, phase, _, d, _ = message
        key = self.orders[stream][phase], d
        link[key] = max(now, link.get(key, 0.0)) + self.unit * self.tiles[stream] * (self.ring(stream, 0) if phase == 2 else 1)
        return link[key] + self.latency

    def offset(self, message):
        stream, phase, _, d, hop = message
        n = self.ring(stream, phase)
        return n // 2 if 2 * hop == n else -d * hop


class Back(Plan):
    def __init__(self, *args):
        super().__init__(*args)
        messages = list(reversed(self.arrived))
        self.needs = {m: self.needed(m) for m in messages}
        self.first = [m for m in messages if not self.needs[m]]
        link, done, came = {}, set(), []
        ready = [(0.0, i, m) for i, m in enumerate(messages) if not self.needs[m]]
        rank = {m: i for i, m in enumerate(messages)}
        pending, started = [], set(self.first)
        while ready or pending:
            if ready and (not pending or ready[0][0] <= pending[0][0]):
                now, i, message = heapq.heappop(ready)
                heapq.heappush(pending, (self.sent(link, now, message), i, message))
                continue
            now, _, message = heapq.heappop(pending)
            done.add(message)
            came.append(message)
            self.time[message] = now
            self.after[message] = [m for m in messages if m not in started and self.needs[m] <= done]
            for m in self.after[message]:
                started.add(m)
                heapq.heappush(ready, (now, rank[m], m))
        self.arrived = came

    def needed(self, message):
        stream, phase, piece, d, hop = message
        off = self.offset(message)
        needs = set()
        if hop < dict(self.ways(stream, phase, piece))[d]:
            needs.add((stream, phase, piece, d, hop + 1))
        if phase < 2:
            needs |= {(stream, phase + 1, off, way, 1) for way, _ in self.ways(stream, phase + 1, off)}
        if phase == 0:
            needs |= {(stream, 2, 0, way, 1) for way, _ in self.ways(stream, 2, 0)}
        return needs


def dot(a, b, dims):
    return lax.dot_general(a, b, (dims, ((), ())), preferred_element_type=jnp.float32)


def layer_kernel(dims, plan, back, kept,
                 tok_hbm, grad_hbm, ids_hbm, gates_hbm, wg_hbm, wu_hbm, wd_hbm,
                 g_ref, out_ref, gate_hbm, up_hbm, down_hbm,
                 tok_ref, grad_ref, ids_ref, gates_ref, block, got, both, wg_ref, wu_ref, wd_ref, wcat, stage, acc, c_ref,
                 dcat, turned, tiles_ref, grads_ref, sums, own, land, last,
                 in_sem, weight_sem, half_sem, wsend, wrecv, pair_send, pair_recv, local,
                 send, recv, sib_send, sib_recv, xsend, xrecv, first_send, first_recv, load_sem, dsend, drecv, bsend, brecv, tile_sem, grad_sem, end_send, end_recv):
    units, width = wg_ref.shape
    half = width // 2
    micro = tok_ref.shape[0]
    tiles = plan.tiles
    starts = [0, tiles[0] * LANES, (tiles[0] + kept) * LANES]
    seq, expert, rep = lax.axis_index("seq"), lax.axis_index("expert"), lax.axis_index("rep")
    core = lax.rem(seq, 2)
    place = (2 * (expert // dims[2]) + rep, seq // 2, lax.rem(expert, dims[2]))

    def many(pairs, sem):
        return [pltpu.make_async_copy(a, b, sem.at[i]) for i, (a, b) in enumerate(pairs)]

    inputs = many(((tok_hbm, tok_ref), (grad_hbm, grad_ref), (ids_hbm, ids_ref), (gates_hbm, gates_ref)), in_sem)
    weights = many(((wg_hbm, wg_ref), (wu_hbm, wu_ref), (wd_hbm, wd_ref)), weight_sem)
    mine_half = pl.ds(pl.multiple_of(core * half, LANES), half)
    other_half = pl.ds(pl.multiple_of((1 - core) * half, LANES), half)
    halves = many(((wg_hbm.at[:, mine_half], wcat.at[pl.ds(0, units)]), (wu_hbm.at[:, mine_half], wcat.at[pl.ds(units, units)])), half_sem)
    for copy in inputs:
        copy.start()

    def device(at, which):
        x, y, z = at
        return {"seq": 2 * y + which, "expert": (x // 2) * dims[2] + z, "rep": lax.rem(x, 2)}

    def shifted(axis, offset):
        return lax.rem(place[axis] + offset + dims[axis], dims[axis])

    def neighbour(axis, d):
        at = list(place)
        at[axis] = shifted(axis, d)
        return device(at, core)

    sibling = device(place, 1 - core)
    around = [sibling] + [neighbour(axis, d) for axis in range(3) for d in (1, -1)] + [neighbour(0, 2)]
    barrier = pltpu.get_barrier_semaphore()
    for other in around:
        pl.semaphore_signal(barrier, inc=1, device_id=other, device_id_type=MESH)
    for copy in inputs:
        copy.wait()

    rows_of = lambda ref: jnp.concatenate([ref[m].astype(jnp.float32) for m in range(micro)], axis=0)
    ids = jnp.concatenate([ids_ref[m] for m in range(micro)], axis=0)
    gates = rows_of(gates_ref)
    lane = lax.broadcasted_iota(jnp.int32, (ids.shape[0], LANES), 1)
    coeff = jnp.zeros(lane.shape, jnp.float32)
    for k in range(ids.shape[1]):
        coeff = coeff + jnp.where(lane == ids[:, k:k + 1], gates[:, k:k + 1], 0.0)
    block[:, :width] = jnp.concatenate([rows_of(tok_ref), rows_of(grad_ref)], axis=0).astype(jnp.bfloat16)
    block[:, width:] = jnp.concatenate([coeff, jnp.zeros_like(coeff)], axis=0).astype(jnp.bfloat16)
    pl.semaphore_wait(barrier, len(around))

    pair = pltpu.make_async_remote_copy(
        src_ref=block, dst_ref=got, send_sem=pair_send, recv_sem=pair_recv, device_id=sibling, device_id_type=MESH)
    pair.start()
    for copy in weights + halves:
        copy.start()
    pair.wait()
    mine, other = block[...].astype(jnp.float32), got[...].astype(jnp.float32)
    first = jnp.where(core == 0, mine, other)
    second = jnp.where(core == 0, other, mine)
    rows = block.shape[0] // 2
    upper = jnp.concatenate([first[:rows], second[:rows]], axis=0)
    lower = jnp.concatenate([first[rows:], second[rows:]], axis=0)
    both[...] = jnp.where(core == 0, upper, lower).astype(jnp.bfloat16)
    spot = (place[0] // 2, place[1], place[2])
    sizes = (2,) + dims[1:]
    west = lax.rem(spot[0] + 1 + rep, 2)
    copy = pltpu.make_async_copy(both, g_ref.at[(core, 0) + spot], local)
    copy.start()
    copy.wait()

    def moved(axis, offset, base=None):
        return lax.rem((spot[axis] if base is None else base) + offset + sizes[axis], sizes[axis])

    def turn(axis, d):
        return neighbour(axis, 2 if axis == 0 else d)

    def lanes_of(stream, crossing=False):
        return pl.ds(starts[stream], (kept if crossing and stream == 1 else tiles[stream]) * LANES)

    def chunk(stream, phase, piece, offset):
        a, b, c = ORDERS[stream]
        at = [None] * 3
        base = west if stream == 2 else None
        if phase == 0:
            at[a], at[b], at[c] = moved(a, offset, base), spot[b], spot[c]
        elif phase == 1:
            at[a], at[b], at[c] = moved(a, piece, base), moved(b, offset), spot[c]
        else:
            at[a], at[b], at[c] = slice(None), slice(None) if piece is None else moved(b, piece), moved(c, offset)
        return tuple(at)

    def place_in(which, group, stream, at, crossing=False):
        return g_ref.at[(which, group) + at + (slice(None), lanes_of(stream, crossing))]

    number = {message: i for i, message in enumerate(plan.arrived)}

    def ring(message, incoming):
        stream, phase, piece, d, hop = message
        if stream == 2 and phase == 0:
            target = place_in(core, 1, 2, chunk(2, 0, 0, -1) if incoming else spot)
            i = number[message]
            return pltpu.make_async_remote_copy(
                src_ref=place_in(core, 0, 2, spot), dst_ref=target, send_sem=send.at[i], recv_sem=recv.at[i],
                device_id=neighbour(0, -1), device_id_type=MESH)
        ref = place_in(core, stream // 2, stream, chunk(stream, phase, piece, -d * (hop if incoming else hop - 1)))
        i = number[message]
        return pltpu.make_async_remote_copy(
            src_ref=ref, dst_ref=ref, send_sem=send.at[i], recv_sem=recv.at[i],
            device_id=turn(ORDERS[stream][phase], d), device_id_type=MESH)

    units_in = sorted(((plan.time[m], u) for m in plan.arrived for u in plan.whole[m]), key=lambda pair: pair[0])
    crossing = [u for _, u in units_in if u[0] < 2]
    ready_at = {u: t for t, u in units_in}
    side = {u: 1 if i % 2 == 0 else -1 for i, u in enumerate(crossing)}
    order_of = {u: i for i, u in enumerate(crossing)}
    cross_time, busy = {}, {1: 0.0, -1: 0.0}
    for u in crossing:
        size = 2 * (kept if u[0] == 1 else tiles[u[0]]) * plan.unit
        busy[side[u]] = max(busy[side[u]], ready_at[u]) + size
        cross_time[u] = busy[side[u]] + plan.latency

    def cross(u):
        stream, piece, offset = u
        at = chunk(stream, 2, piece, offset)
        i = order_of[u]
        return pltpu.make_async_remote_copy(
            src_ref=place_in(core, 0, stream, at, True), dst_ref=place_in(core, 1, stream, at, True),
            send_sem=xsend.at[i], recv_sem=xrecv.at[i], device_id=neighbour(0, side[u]), device_id_type=MESH)

    copies = [(0, u) for u in crossing] + [(1, u) for u in crossing] + [(1, u) for _, u in units_in if u[0] == 2]
    place_of = {copy: i for i, copy in enumerate(copies)}

    def across(copy, incoming):
        group, (stream, piece, offset) = copy
        ref = place_in(1 - core if incoming else core, group, stream, chunk(stream, 2, piece, offset), group == 1)
        i = place_of[copy]
        return pltpu.make_async_remote_copy(
            src_ref=ref, dst_ref=ref, send_sem=sib_send.at[i], recv_sem=sib_recv.at[i],
            device_id=sibling, device_id_type=MESH)

    due = {}
    for group, u in copies:
        key = group, u[0], u[2]
        due[key] = max(due.get(key, 0.0), ready_at[u] if group == 0 or u[0] == 2 else cross_time[u])
    tasks = sorted(due, key=lambda key: due[key])

    def shape_of(stream):
        return 2, dims[ORDERS[stream][1]]

    def fetch(task):
        group, stream, offset = task
        slot = tasks.index(task) % 2
        one, two = shape_of(stream)
        return [pltpu.make_async_copy(
            place_in(which, group, stream, chunk(stream, 2, None, offset), group == 1),
            stage.at[slot, which, :, pl.ds(0, two), :, pl.ds(0, lanes_of(stream, group == 1).size)],
            load_sem.at[slot, which]) for which in (0, 1)]

    def load(task):
        for copy in copies:
            if (copy[0], copy[1][0], copy[1][2]) == task:
                across(copy, True).wait_recv()
        for copy in fetch(task):
            copy.start()

    def compute(task):
        group, stream, offset = task
        slot = tasks.index(task) % 2
        one, two = shape_of(stream)
        for copy in fetch(task):
            copy.wait()
        where = chunk(stream, 2, None, offset)
        columns = lanes_of(stream, group == 1).size
        depth = min(columns, width - starts[stream])
        part = pl.ds(starts[stream], depth)
        x, dy = (stage[slot, which, :, pl.ds(0, two), :, pl.ds(0, columns)].reshape(-1, columns) for which in (0, 1))
        for j, (rows, w) in enumerate(((x, wg_ref), (x, wu_ref), (dy, wd_ref))):
            value = dot(rows[:, :depth], w[:, part], ((1,), (1,))).reshape(one, two, 16, units)
            acc[(j, group) + where] = acc[(j, group) + where] + value
        if columns > depth:
            lane = lax.broadcasted_iota(jnp.int32, (one * two * 16, LANES), 1)
            picked = jnp.where(lane == expert, x[:, depth:].astype(jnp.float32), 0.0)
            c_ref[(group,) + where] = jnp.sum(picked, axis=1, keepdims=True).reshape(one, two, 16, 1)

    opening = pltpu.make_async_remote_copy(
        src_ref=place_in(core, 0, 2, spot), dst_ref=place_in(core, 1, 2, spot), send_sem=first_send, recv_sem=first_recv,
        device_id=neighbour(0, 1), device_id_type=MESH)
    opening_in = pltpu.make_async_remote_copy(
        src_ref=place_in(core, 0, 2, spot), dst_ref=place_in(core, 1, 2, (west,) + spot[1:]), send_sem=first_send, recv_sem=first_recv,
        device_id=neighbour(0, 1), device_id_type=MESH)

    rows = 2 * dims[2] * 16

    def activate(group, x, y):
        part = lambda ref: ref[group, x, pl.ds(y, 2)].reshape(rows, ref.shape[-1])
        c = part(c_ref)
        gate_pre, up_pre, d_hidden = (part(acc.at[j]) for j in range(3))
        d_hidden = c * d_hidden
        sigma = jax.nn.sigmoid(gate_pre)
        active = gate_pre * sigma
        hidden = c * (active * up_pre)
        d_up = d_hidden * active
        d_gate = d_hidden * up_pre * sigma * (1.0 + gate_pre * (1.0 - sigma))
        if group == 0:
            for j, value in enumerate((d_gate, d_up)):
                dcat[x, pl.ds(y, 2), :, :, j * units:(j + 1) * units] = value.astype(jnp.bfloat16).reshape(2, dims[2], 16, units)
        at = pl.ds((x * dims[1] + y) * dims[2] * 16, rows)
        for j, value in enumerate((d_gate, d_up, hidden)):
            turned[group, j * units:(j + 1) * units, at] = value.T.astype(jnp.bfloat16)

    def swap(i):
        return pltpu.make_async_remote_copy(
            src_ref=dcat.at[i, :, :, :, pl.ds(0, 2 * units)], dst_ref=dcat.at[i, :, :, :, pl.ds(2 * units, 2 * units)],
            send_sem=dsend.at[i], recv_sem=drecv.at[i], device_id=sibling, device_id_type=MESH)

    back_starts = (0, back.tiles[0] * LANES)
    def lanes(stream):
        return pl.ds(back_starts[stream], back.tiles[stream] * LANES)

    def region(stream, phase, piece, offset):
        a, b, c = BACK[stream]
        at = [None] * 3
        if phase == 0:
            at[a], at[b], at[c] = moved(a, offset), spot[b], spot[c]
        elif phase == 1:
            at[a], at[b], at[c] = moved(a, piece), moved(b, offset), spot[c]
        else:
            at[a], at[b], at[c] = slice(None), moved(b, piece), moved(c, offset)
        return tuple(at) + (slice(None), lanes(stream))

    rank = {message: i for i, message in enumerate(back.arrived)}

    def landing(message):
        stream, phase = message[:2]
        ref = land.at[rank[message]]
        columns = pl.ds(0, back.tiles[stream] * LANES)
        return ref.at[:, :, columns] if phase == 2 else ref.at[0, :, columns]

    def hand(message):
        stream, phase, piece, d, hop = message
        i = rank[message]
        axis = BACK[stream][phase]
        return pltpu.make_async_remote_copy(
            src_ref=own.at[region(stream, phase, piece, -d * hop)], dst_ref=landing(message), send_sem=bsend.at[i], recv_sem=brecv.at[i],
            device_id=turn(axis, -d), device_id_type=MESH)

    def make(i):
        swap(i).wait_recv()
        rows = dcat[i].reshape(-1, 4 * units)
        wide = min(512, half)

        @pl.loop(0, half // wide)
        def _(k):
            cols = pl.ds(pl.multiple_of(k * wide, wide), wide)
            value = dot(rows, wcat[:, cols], ((1,), (0,)))
            own[i, :, :, :, cols] = value.astype(jnp.bfloat16).reshape(dims[1], dims[2], 16, wide)

    width_of = tiles_ref.shape[-1]
    count = width // width_of

    def tile(group, i):
        cols = pl.ds(i * width_of, width_of)
        return [pltpu.make_async_copy(g_ref.at[which, group, :, :, :, :, cols], tiles_ref.at[i % 2, which], tile_sem.at[i % 2, which]) for which in (0, 1)]

    def result(i):
        cols = pl.ds(i * width_of, width_of)
        return [pltpu.make_async_copy(grads_ref.at[i % 2, pl.ds(j * units, units)], ref.at[:, cols], grad_sem.at[i % 2, j])
                for j, ref in enumerate((gate_hbm, up_hbm, down_hbm))]

    def weigh(group, i):
        if i == 0:
            for copy in tile(group, 0):
                copy.start()
        if i + 1 < count:
            for copy in tile(group, i + 1):
                copy.start()
        for copy in tile(group, i):
            copy.wait()
        if group == 1 and i >= 2:
            for copy in result(i - 2):
                copy.wait()
        x, dy = (tiles_ref[i % 2, which].reshape(-1, width_of) for which in (0, 1))
        cols = pl.ds(i * width_of, width_of)
        for low, high, rows in ((0, 2 * units, x), (2 * units, 3 * units, dy)):
            value = dot(turned[group, low:high], rows, ((1,), (0,)))
            if group == 0:
                sums[low:high, cols] = value
            else:
                grads_ref[i % 2, low:high] = (sums[low:high, cols] + value).astype(jnp.bfloat16)
        if group == 1:
            for copy in result(i):
                copy.start()

    opening.start()
    for message in plan.first:
        if message[0] < 2 or message[1] == 0:
            ring(message, False).start()
    acc[...] = jnp.zeros_like(acc)
    for copy in weights + halves:
        copy.wait()
    lent = [pltpu.make_async_remote_copy(
        src_ref=ref.at[:, other_half], dst_ref=wcat.at[pl.ds((2 + i) * units, units)], send_sem=wsend.at[i], recv_sem=wrecv.at[i],
        device_id=sibling, device_id_type=MESH) for i, ref in enumerate((wg_ref, wu_ref))]
    for copy in lent:
        copy.start()

    waiting, flying = {1: [], -1: []}, {1: 0, -1: 0}

    def cross_more(d):
        while waiting[d] and flying[d] < 99:
            cross(waiting[d].pop(0)).start()
            flying[d] += 1

    loaded = []

    def begin_task(task):
        load(task)
        finish_task()
        loaded.append(task)

    def finish_task():
        if loaded:
            compute(loaded.pop())

    def on_ring(message):
        ring(message, True).wait_recv()
        for later in plan.after[message]:
            ring(later, False).start()
        for u in plan.whole[message]:
            across((u[0] // 2, u), False).start()
            if u[0] < 2:
                waiting[side[u]].append(u)
                cross_more(side[u])

    def on_cross(u):
        cross(u).wait_recv()
        across((1, u), False).start()
        flying[side[u]] -= 1
        cross_more(side[u])

    def on_opening():
        opening_in.wait_recv()
        for message in plan.first:
            if message[0] == 2 and message[1] > 0:
                ring(message, False).start()

    def on_swap():
        for copy in lent:
            copy.wait()
        make(0)

    def on_first(message):
        hand(message).start()

    def on_back(message):
        hand(message).wait_recv()
        stream, phase, piece, d, hop = message
        at = region(stream, phase, piece, -d * (hop - 1))
        own[at] = own[at] + landing(message)[...]
        for later in back.after[message]:
            hand(later).start()

    end = pltpu.make_async_remote_copy(
        src_ref=own.at[spot], dst_ref=last, send_sem=end_send, recv_sem=end_recv, device_id=sibling, device_id_type=MESH)
    act = functools.partial
    line = [(plan.time[m], act(on_ring, m)) for m in plan.arrived]
    line += [(cross_time[u], act(on_cross, u)) for u in crossing]
    line += [(min(plan.time[m] for m in plan.arrived if m[0] == 2) - 0.01, on_opening)]
    line += [(due[task] + 4.0, act(begin_task, task)) for task in tasks]
    settled = max(due[task] for task in tasks if task[0] == 0) + 4.0
    steps = [finish_task, act(activate, 0, 0, 0), act(activate, 0, 0, 2), lambda: swap(0).start(),
             act(activate, 0, 1, 0), act(activate, 0, 1, 2), lambda: swap(1).start()]
    line += [(settled + 0.01 + 0.8 * i, step) for i, step in enumerate(steps)]
    go = settled + 9.0
    line += [(go - 2.0, on_swap), (go - 0.01, act(make, 1))]
    line += [(go + 0.1 * i, act(on_first, m)) for i, m in enumerate(back.first)]
    base = go + 0.1 * len(back.first)
    line += [(base + back.time[m], act(on_back, m)) for m in back.arrived]
    finish = base + max(back.time.values())
    line += [(finish + 0.01, end.start)]
    line += [(base + 1.0 + (finish - base) * i / count, act(weigh, 0, i)) for i in range(count)]
    for _, step in sorted(line, key=lambda pair: pair[0]):
        step()
    finish_task()
    for x in range(2):
        for y in range(0, dims[1], 2):
            activate(1, x, y)
    for i in range(count):
        weigh(1, i)

    for copy in copies:
        across(copy, False).wait_send()
    for message in plan.arrived:
        ring(message, False).wait_send()
    for u in crossing:
        cross(u).wait_send()
    opening.wait_send()
    for message in back.arrived:
        hand(message).wait_send()
    for i in (0, 1):
        swap(i).wait_send()
    end.wait()
    mine = own[spot].astype(jnp.float32)
    other = last[...].astype(jnp.float32)
    rows = mine.shape[0] // 2
    left_half = jnp.where(core == 0, mine[:rows], other[rows:])
    right_half = jnp.where(core == 0, other[:rows], mine[rows:])
    each = out_ref.shape[1]
    for m in range(micro):
        out_ref[m, :, :half] = left_half[m * each:(m + 1) * each].astype(jnp.bfloat16)
        out_ref[m, :, half:] = right_half[m * each:(m + 1) * each].astype(jnp.bfloat16)
    for i in range(max(0, count - 2), count):
        for copy in result(i):
            copy.wait()


def layer(dims, tokens, grad_out, ids, gates, wg, wu, wd):
    units, width = wg.shape
    columns = width + LANES
    half = width // 2
    n = columns // LANES
    late = max(2, n * 5 // 33)
    first = n * 14 // 33
    kept = n - first - late
    grid = (2,) + dims[1:]
    quiet = max(Plan(grid, ORDERS[:2], (first, n - first)).time.values()) - 6.0
    plan = Plan(grid, ORDERS, (first, n - first, late), (0.0, 0.0, quiet))
    narrow = half // LANES * 7 // 16
    back = Back(grid, BACK, (narrow, half // LANES - narrow))
    count, back_count = len(plan.arrived), len(back.arrived)
    units_in = [u for m in plan.arrived for u in plan.whole[m]]
    crossed = sum(1 for u in units_in if u[0] < 2)
    passed = len(units_in) + crossed
    local = 2 * tokens.shape[0] * tokens.shape[1]
    total = dims[0] * dims[1] * dims[2] * 16
    tile = min(512, width)
    bf16 = lambda *shape: pltpu.VMEM(shape, jnp.bfloat16)
    like = lambda a: pltpu.VMEM(a.shape, a.dtype)
    sems = lambda *n: pltpu.SemaphoreType.DMA(n)
    one = pltpu.SemaphoreType.DMA
    vmem, hbm = pl.BlockSpec(memory_space=pltpu.VMEM), pl.BlockSpec(memory_space=pl.ANY)
    grad = jax.ShapeDtypeStruct((units, width), jnp.bfloat16)
    return pl.pallas_call(
        functools.partial(layer_kernel, dims, plan, back, kept),
        out_shape=(
            jax.ShapeDtypeStruct((2, 2) + grid + (16, columns), jnp.bfloat16),
            jax.ShapeDtypeStruct(tokens.shape, jnp.bfloat16),
            grad, grad, grad,
        ),
        in_specs=[hbm] * 7,
        out_specs=(hbm, vmem, hbm, hbm, hbm),
        scratch_shapes=[
            like(tokens), like(grad_out), like(ids), like(gates),
            bf16(local, columns), bf16(local, columns), bf16(local, columns),
            bf16(units, width), bf16(units, width), bf16(units, width),
            bf16(4 * units, half),
            bf16(2, 2, 2, max(dims[1:]), 16, max(plan.tiles) * LANES),
            pltpu.VMEM((3, 2) + grid + (16, units), jnp.float32),
            pltpu.VMEM((2,) + grid + (16, 1), jnp.float32),
            bf16(2, dims[1], dims[2], 16, 4 * units),
            bf16(2, 3 * units, total // 2),
            bf16(2, 2, *grid, 16, tile),
            bf16(2, 3 * units, tile),
            pltpu.VMEM((3 * units, width), jnp.float32),
            bf16(2, dims[1], dims[2], 16, half),
            bf16(back_count, 2, 16, max(back.tiles) * LANES),
            bf16(16, half),
            sems(4), sems(3), sems(2), sems(2), sems(2), one, one, one,
            sems(count), sems(count), sems(passed), sems(passed), sems(crossed), sems(crossed), one, one, sems(2, 2),
            sems(2), sems(2), sems(back_count), sems(back_count), sems(2, 2), sems(2, 3), one, one,
        ],
        compiler_params=pltpu.CompilerParams(collective_id=0, has_side_effects=True, vmem_limit_bytes=60 << 20),
    )(tokens, grad_out, ids, gates, wg, wu, wd)


def body(tokens, grad_out, expert_ids, gate_weights, w_gate, w_up, w_down):
    dims = (2 * lax.axis_size("rep"), lax.axis_size("seq") // 2, lax.axis_size("expert") // 2)
    _, d_tokens, *grads = layer(dims, tokens, grad_out, expert_ids, gate_weights, w_gate[0], w_up[0], w_down[0])
    return (d_tokens,) + tuple(g[None] for g in grads)


def solution(mesh):
    rows = P(None, ALL, None)
    weights = P("expert", "seq", None)
    return jax.shard_map(
        body,
        mesh=mesh,
        in_specs=(rows, rows, rows, rows, weights, weights, weights),
        out_specs=(rows, weights, weights, weights),
        check_vma=False,
    )
```

time: 164 us -> 158 us (0.963); the launches traced: 163 us -> 155 us
  Pallas kernels: 155 us -> 147 us
    pallas_call x1, Pallas kernels: 155 us -> 147 us  [layer(): pl.pallas_call(functools.partial(layer_kernel, dims, plan, back, kept), o...]
where the time goes in v3:
time: 158 us; the launch traced here: 155 us
  Pallas kernels  147 us (93%)
  local copies, waits for them, and re-layouts  7.43 us (5%)
    pallas_call x1, Pallas kernels, layer(): pl.pallas_call(functools.partial(layer_kernel, dims, plan, back, kept), o...  147 us
    unnamed x8, local copies, waits for them, and re-layouts  7.43 us

profile of v3, /device:TPU:1, one launch (start us, length us, event | category | flops | bytes accessed | tf_op | source)
XLA Modules:
  0.0 155.0 jit_solution(11896656577678493548)
XLA Ops:
  0.6 146.9 %shard_map.102 = (bf16[2,2,2,4,8,16,4224]{6,5,4,3,2,1,0:T(8,128)(2,1)}, bf16[2,4,4096]{2,1,0:T(4,128)(2,1)}, bf16[192,4096]{1,0:T(8,128)(2,1)}, bf16[192,4096]{1,0:T(8,128)(2,1)}, bf16[192,4096]{1,0:T(8,128)(2,1)}) custom-call(bf16[2,4,4096]{2,1,0:T(4,128)(2,1)} %tok_hbm.1, bf16[2,4,4096]{2,1,0:T(4,128)(2,1)} %grad_hbm.1, s32[2,4,8]{2,1,0:T(4,128)} %ids_hbm.1, ...), custom_call_target="tpu_custom_call" | custom-call | tf_op jit(solution)/shard_map/pallas_call | solution.py:580
  147.5 1.5 copy.15
  149.0 0.0 copy-start.1
  149.0 2.8 %copy.16 = bf16[1,192,4096]{2,1,0:T(8,128)(2,1)} copy(bf16[1,192,4096]{2,1,0:T(8,128)(2,1)} %bitcast.11) | data formatting | bytes 3145728
  151.8 0.0 copy-done.1
  151.8 0.0 copy-start
  151.8 1.1 copy.17
  153.0 0.8 copy-done
  153.8 1.1 copy.18
Async XLA Ops:
  149.0 2.8 %copy-start.1 = (bf16[192,4096]{1,0:T(8,128)(2,1)S(1)}, bf16[192,4096]{1,0:T(8,128)(2,1)}, u32[]{:S(2)}) copy-start(bf16[192,4096]{1,0:T(8,128)(2,1)} %get-tuple-element.10) | copy-start | bytes 4718596
  151.8 2.0 %copy-start = (bf16[192,4096]{1,0:T(8,128)(2,1)S(1)}, bf16[192,4096]{1,0:T(8,128)(2,1)}, u32[]{:S(2)}) copy-start(bf16[192,4096]{1,0:T(8,128)(2,1)} %get-tuple-element.11) | copy-start | bytes 4718596
